TPU v7x, 128 devices: a whole 4x4x4 slice. The times are simulated.
128 devices in a mesh: ctx: 8 (over x_hi, z), fsdp: 16 (over y, x_lo, core).
Axes of the slice: x: 4 (x_hi: 2, x_lo: 2; x = x_hi * 2 + x_lo), y: 4, z: 4, core: 2. Of those that a mesh axis runs over, the one named last changes fastest.
Arguments:
- tokens: bfloat16 [32, 1024, 1024], P('fsdp', 'ctx'), may hold values from -6 to 6
- span_order: int32 [32, 16], P('fsdp'), may hold values from 0 to 15, as said below
- w_query: bfloat16 [1024, 2048], P('fsdp'), may hold values from -0.1875 to 0.1875
- w_key: bfloat16 [1024, 1024], P('fsdp'), may hold values from -0.1875 to 0.1875
- w_value: bfloat16 [1024, 1024], P('fsdp'), may hold values from -0.1875 to 0.1875
- w_out: bfloat16 [2048, 1024], P('fsdp'), may hold values from -0.125 to 0.125
- w_gate: bfloat16 [1024, 3072], P('fsdp'), may hold values from -0.1875 to 0.1875
- w_up: bfloat16 [1024, 3072], P('fsdp'), may hold values from -0.1875 to 0.1875
- w_down: bfloat16 [3072, 1024], P('fsdp'), may hold values from -0.109375 to 0.109375
- query_gain: float32 [2048], P('fsdp'), may hold values from 0.1 to 1.9
- key_gain: float32 [1024], P('fsdp'), may hold values from 0.1 to 1.9
- attn_gain: float32 [1024], P('fsdp'), may hold values from 0.1 to 1.9
- ffn_gain: float32 [1024], P('fsdp'), may hold values from 0.1 to 1.9
- cotangent: bfloat16 [32, 1024, 1024], P('fsdp', 'ctx'), may hold values from -6 to 6
Outputs:
- layer_out: bfloat16 [32, 1024, 1024], P('fsdp', 'ctx')
- grad_tokens: bfloat16 [32, 1024, 1024], P('fsdp', 'ctx')
- grad_w_query: float32 [1024, 2048], P('fsdp')
- grad_w_key: float32 [1024, 1024], P('fsdp')
- grad_w_value: float32 [1024, 1024], P('fsdp')
- grad_w_out: float32 [2048, 1024], P('fsdp')
- grad_w_gate: float32 [1024, 3072], P('fsdp')
- grad_w_up: float32 [1024, 3072], P('fsdp')
- grad_w_down: float32 [3072, 1024], P('fsdp')
- grad_query_gain: float32 [2048], P('fsdp')
- grad_key_gain: float32 [1024], P('fsdp')
- grad_attn_gain: float32 [1024], P('fsdp')
- grad_ffn_gain: float32 [1024], P('fsdp')
Inputs may be any that keep to these rules, and one draw needn't show every extreme that they name: `span_order`: each row is a permutation of the 16 block numbers in which slots 2 c and 2 c + 1 hold blocks p and 15 - p for some p, so that every index of ctx holds one early and one late block of each sequence.
All inputs are finite; a program needn't handle non-finite values.
Results may differ from a plain program's by a relative error of at most 0.028.
Values may be sent and summed in bfloat16 or wider, within the bound.
A program may use at most 256 MiB of HBM per device.

v0:
```python
import jax
import jax.numpy as jnp
from jax import lax
from jax.sharding import PartitionSpec as P

HEADS = 16
HEAD = 128
KV_HEADS = 8


rope_base = 1000000.0
norm_eps = 1e-06


def in_blocks(array, dim, devices):
    before, after = (array.shape[:dim], array.shape[dim + 1 :])
    return jnp.moveaxis(array.reshape(*before, devices, -1, *after), dim, 0)


def sent_and_summed(array, axis, dim):
    pieces = in_blocks(array, dim, lax.axis_size(axis))
    arrived = lax.all_to_all(pieces, axis, split_axis=0, concat_axis=0, tiled=True)
    return arrived.astype(jnp.float32).sum(axis=0)


def sent_together(arrays, axis, dim, along):
    ends, at = ([], 0)
    for a in arrays[:-1]:
        at += a.shape[along]
        ends.append(at)
    both = jnp.concatenate(arrays, axis=along)
    return tuple(jnp.split(lax.all_gather(both, axis, axis=dim, tiled=True), ends, axis=along))


def packed_total(arrays, axis):
    ends = [0]
    for a in arrays:
        ends.append(ends[-1] + a.size)
    so_far = lax.psum(jnp.concatenate([a.ravel() for a in arrays]), axis)
    return tuple((so_far[b:e].reshape(a.shape) for a, b, e in zip(arrays, ends, ends[1:])))


def rms_forward(values, norm_gain):
    inverse = lax.rsqrt(jnp.mean(values * values, -1, keepdims=True) + norm_eps)
    return (values * inverse * norm_gain, inverse)


def rms_backward(values, inverse, norm_gain, upstream):
    scaled = upstream * norm_gain
    row_inner = jnp.mean(scaled * values, -1, keepdims=True)
    grad_values = inverse * scaled - values * (inverse * inverse * inverse) * row_inner
    grad_gain = jnp.sum(upstream * values * inverse, 0)
    return (grad_values, grad_gain)


def angles(positions):
    steps_half = jnp.arange(HEAD // 2, dtype=jnp.float32)
    inverse_freq = rope_base ** (-2.0 * steps_half / HEAD)
    phase = positions.astype(jnp.float32)[..., None] * inverse_freq
    phase = jnp.concatenate([phase, phase], -1)
    return (jnp.cos(phase), jnp.sin(phase))


def rotate(values, cosine, sine):
    half_width = values.shape[-1] // 2
    turned = jnp.concatenate([-values[..., half_width:], values[..., :half_width]], -1)
    return values * cosine + turned * sine


def fold_rows(left_rows, stacked):
    return jnp.dot(
        left_rows,
        lax.all_gather(stacked, "fsdp", axis=0, tiled=True),
        preferred_element_type=jnp.float32,
    )


def fold_back(grad_rows, stacked):
    return lax.dot_general(
        grad_rows,
        lax.all_gather(stacked, "fsdp", axis=0, tiled=True),
        (((1,), (1,)), ((), ())),
        preferred_element_type=jnp.float32,
    )


def weight_grad(left_rows, grad_rows):
    return sent_and_summed(
        lax.dot_general(
            left_rows, grad_rows, (((0,), (0,)), ((), ())), preferred_element_type=jnp.float32
        ).astype(jnp.bfloat16),
        "fsdp",
        0,
    )


def per_device(
    tokens,
    span_order,
    w_query,
    w_key,
    w_value,
    w_out,
    w_gate,
    w_up,
    w_down,
    query_gain,
    key_gain,
    attn_gain,
    ffn_gain,
    cotangent,
):
    ctx_count = lax.axis_size("ctx")
    seq_local, rows_local, width = tokens.shape
    span_rows = rows_local // 2
    total_rows = seq_local * rows_local
    group_size = HEADS // KV_HEADS
    query_width = HEADS * HEAD
    key_width = KV_HEADS * HEAD
    ffn_width = w_gate.shape[1]
    score_scale = HEAD ** (-0.5)
    token_rows = tokens.reshape(total_rows, width)
    qkv_stack = jnp.concatenate([w_query, w_key, w_value], 1)
    gate_stack = jnp.concatenate([w_gate, w_up], 1)
    q_gain_all, k_gain_all, a_gain_all, f_gain_all = (
        lax.all_gather(query_gain, "fsdp", axis=0, tiled=True),
        lax.all_gather(key_gain, "fsdp", axis=0, tiled=True),
        lax.all_gather(attn_gain, "fsdp", axis=0, tiled=True),
        lax.all_gather(ffn_gain, "fsdp", axis=0, tiled=True),
    )
    ctx_index = lax.axis_index("ctx")
    own_spans = lax.dynamic_slice_in_dim(span_order, 2 * ctx_index, 2, 1)
    offsets = jnp.arange(span_rows, dtype=jnp.int32)
    query_pos = (own_spans[:, :, None] * span_rows + offsets).reshape(seq_local, rows_local)
    key_pos = (span_order[:, :, None] * span_rows + offsets).reshape(
        seq_local, 2 * ctx_count * span_rows
    )
    visible = key_pos[:, None, :] <= query_pos[:, :, None]
    cosine, sine = angles(query_pos)
    cosine = cosine[:, :, None, :]
    sine = sine[:, :, None, :]
    qkv_raw = fold_rows(token_rows, qkv_stack)
    query_raw = qkv_raw[:, :query_width]
    key_raw = qkv_raw[:, query_width : query_width + key_width]
    value_raw = qkv_raw[:, query_width + key_width :]
    query_normed, query_inverse = rms_forward(query_raw, q_gain_all)
    key_normed, key_inverse = rms_forward(key_raw, k_gain_all)
    query_rot = rotate(query_normed.reshape(seq_local, rows_local, HEADS, HEAD), cosine, sine)
    query_low = query_rot.astype(jnp.bfloat16).reshape(
        seq_local, rows_local, KV_HEADS, group_size, HEAD
    )
    key_low = rotate(
        key_normed.reshape(seq_local, rows_local, KV_HEADS, HEAD), cosine, sine
    ).astype(jnp.bfloat16)
    value_low = value_raw.astype(jnp.bfloat16).reshape(seq_local, rows_local, KV_HEADS, HEAD)
    keys_all, values_all = sent_together((key_low, value_low), "ctx", 1, 0)

    def scores_of():
        raw_scores = jnp.einsum(
            "sqkgd,stkd->skgqt", query_low, keys_all, preferred_element_type=jnp.float32
        )
        return jnp.where(visible[:, None, None], raw_scores * score_scale, -1e30)

    scores = scores_of()
    row_top = jnp.max(scores, -1, keepdims=True)
    raised = jnp.exp(scores - row_top)
    row_total = jnp.sum(raised, -1, keepdims=True)
    log_total = row_top + jnp.log(row_total)
    probs_low = (raised / row_total).astype(jnp.bfloat16)
    attended = jnp.einsum(
        "skgqt,stkd->sqkgd", probs_low, values_all, preferred_element_type=jnp.float32
    )
    attended_low = attended.reshape(total_rows, query_width).astype(jnp.bfloat16)
    branch = fold_rows(attended_low, w_out)
    branch_normed, branch_inverse = rms_forward(branch, a_gain_all)
    mixed = token_rows.astype(jnp.float32) + branch_normed
    mixed_low = mixed.astype(jnp.bfloat16)
    gate_up = fold_rows(mixed_low, gate_stack)
    gate = gate_up[:, :ffn_width]
    upward = gate_up[:, ffn_width:]
    middle_low = (jax.nn.silu(gate) * upward).astype(jnp.bfloat16)
    ffn_out = fold_rows(middle_low, w_down)
    ffn_normed, ffn_inverse = rms_forward(ffn_out, f_gain_all)
    layer_out = (mixed + ffn_normed).astype(jnp.bfloat16).reshape(seq_local, rows_local, width)
    grad_rows_out = cotangent.reshape(total_rows, width).astype(jnp.float32)
    grad_ffn, grad_ffn_gain = rms_backward(ffn_out, ffn_inverse, f_gain_all, grad_rows_out)
    grad_ffn_low = grad_ffn.astype(jnp.bfloat16)
    grad_middle = fold_back(grad_ffn_low, w_down)
    sigmoid_gate = jax.nn.sigmoid(gate)
    grad_gate = grad_middle * upward * sigmoid_gate * (1.0 + gate * (1.0 - sigmoid_gate))
    grad_upward = grad_middle * jax.nn.silu(gate)
    grad_gate_up = jnp.concatenate([grad_gate, grad_upward], 1).astype(jnp.bfloat16)
    grad_mixed = grad_rows_out + fold_back(grad_gate_up, gate_stack)
    grad_branch, grad_attn_gain = rms_backward(branch, branch_inverse, a_gain_all, grad_mixed)
    grad_branch_low = grad_branch.astype(jnp.bfloat16)
    grad_attended = fold_back(grad_branch_low, w_out).astype(jnp.bfloat16)
    grad_attended = grad_attended.reshape(seq_local, rows_local, KV_HEADS, group_size, HEAD)
    probs = jnp.exp(scores_of() - log_total)
    grad_probs = jnp.einsum(
        "sqkgd,stkd->skgqt", grad_attended, values_all, preferred_element_type=jnp.float32
    )
    row_inner = jnp.sum(probs * grad_probs, -1, keepdims=True)
    grad_scores = (probs * (grad_probs - row_inner)).astype(jnp.bfloat16)
    grad_query = (
        jnp.einsum("skgqt,stkd->sqkgd", grad_scores, keys_all, preferred_element_type=jnp.float32)
        * score_scale
    )
    grad_keys_part = (
        jnp.einsum("skgqt,sqkgd->stkd", grad_scores, query_low, preferred_element_type=jnp.float32)
        * score_scale
    )
    grad_values_part = jnp.einsum(
        "skgqt,sqkgd->stkd",
        probs.astype(jnp.bfloat16),
        grad_attended,
        preferred_element_type=jnp.float32,
    )
    grad_keys, grad_values = (
        lax.psum_scatter(
            grad_keys_part.astype(jnp.bfloat16), "ctx", scatter_dimension=1, tiled=True
        ).astype(jnp.float32),
        lax.psum_scatter(
            grad_values_part.astype(jnp.bfloat16), "ctx", scatter_dimension=1, tiled=True
        ).astype(jnp.float32),
    )
    grad_query_rot = rotate(grad_query.reshape(seq_local, rows_local, HEADS, HEAD), cosine, -sine)
    grad_query_raw, grad_query_gain = rms_backward(
        query_raw, query_inverse, q_gain_all, grad_query_rot.reshape(total_rows, query_width)
    )
    grad_key_rot = rotate(grad_keys, cosine, -sine)
    grad_key_raw, grad_key_gain = rms_backward(
        key_raw, key_inverse, k_gain_all, grad_key_rot.reshape(total_rows, key_width)
    )
    grad_qkv = jnp.concatenate(
        [grad_query_raw, grad_key_raw, grad_values.reshape(total_rows, key_width)], 1
    ).astype(jnp.bfloat16)
    grad_tokens = (grad_mixed + fold_back(grad_qkv, qkv_stack)).astype(jnp.bfloat16)
    grad_tokens = grad_tokens.reshape(seq_local, rows_local, width)
    shard_qkv = weight_grad(token_rows, grad_qkv)
    shard_out = weight_grad(attended_low, grad_branch_low)
    shard_gate = weight_grad(mixed_low, grad_gate_up)
    shard_down = weight_grad(middle_low, grad_ffn_low)
    gain_q, gain_k, gain_a, gain_f = (
        lax.psum_scatter(grad_query_gain, "fsdp", scatter_dimension=0, tiled=True),
        lax.psum_scatter(grad_key_gain, "fsdp", scatter_dimension=0, tiled=True),
        lax.psum_scatter(grad_attn_gain, "fsdp", scatter_dimension=0, tiled=True),
        lax.psum_scatter(grad_ffn_gain, "fsdp", scatter_dimension=0, tiled=True),
    )
    summed = tuple(
        (
            part.astype(jnp.float32)
            for part in packed_total(
                (
                    shard_qkv.astype(jnp.bfloat16),
                    shard_out.astype(jnp.bfloat16),
                    shard_gate.astype(jnp.bfloat16),
                    shard_down.astype(jnp.bfloat16),
                    gain_q.astype(jnp.bfloat16),
                    gain_k.astype(jnp.bfloat16),
                    gain_a.astype(jnp.bfloat16),
                    gain_f.astype(jnp.bfloat16),
                ),
                "ctx",
            )
        )
    )
    (
        total_qkv,
        total_out,
        total_gate,
        total_down,
        total_q_gain,
        total_k_gain,
        total_a_gain,
        total_f_gain,
    ) = summed
    return (
        layer_out,
        grad_tokens,
        total_qkv[:, :query_width],
        total_qkv[:, query_width : query_width + key_width],
        total_qkv[:, query_width + key_width :],
        total_out,
        total_gate[:, :ffn_width],
        total_gate[:, ffn_width:],
        total_down,
        total_q_gain,
        total_k_gain,
        total_a_gain,
        total_f_gain,
    )


def solution(mesh):
    in_specs = (
        P("fsdp", "ctx", None),
        P("fsdp", None),
        P("fsdp", None),
        P("fsdp", None),
        P("fsdp", None),
        P("fsdp", None),
        P("fsdp", None),
        P("fsdp", None),
        P("fsdp", None),
        P("fsdp"),
        P("fsdp"),
        P("fsdp"),
        P("fsdp"),
        P("fsdp", "ctx", None),
    )
    out_specs = (
        P("fsdp", "ctx", None),
        P("fsdp", "ctx", None),
        P("fsdp", None),
        P("fsdp", None),
        P("fsdp", None),
        P("fsdp", None),
        P("fsdp", None),
        P("fsdp", None),
        P("fsdp", None),
        P("fsdp"),
        P("fsdp"),
        P("fsdp"),
        P("fsdp"),
    )
    return jax.shard_map(
        per_device, mesh=mesh, in_specs=in_specs, out_specs=out_specs, check_vma=False
    )
```

profile of v0, /device:TPU:0, one launch (start us, length us, event | category | flops | bytes accessed | tf_op | source)
XLA Modules:
  0.0 1004.2 jit_solution(9046354385838253792)
XLA Ops:
  14.7 56.9 %all-reduce.8 = (f32[1024]{0:T(1024)S(1)}, f32[1024]{0:T(1024)S(1)}, f32[1024]{0:T(1024)S(1)}) all-reduce(f32[1024]{0:T(1024)S(1)} %dynamic-update-slice, f32[1024]{0:T(1024)S(1)} %dynamic-update-slice.1, f32[1024]{0:T(1024)S(1)} %dynamic-update-slice.2), channel_id=1, replica_groups=mesh['ctx'=8,'fsdp'=16] {'fsdp'}, use_global_device_ids=true, to_apply=%add | all-reduce | flops 3072 | bytes 24576
  72.9 5.9 convolution_bitcast_fusion
  93.3 15.8 %all-gather = f32[16,1,128]{2,1,0:T(1,128)S(1)} all-gather(f32[1,1,128]{2,1,0:T(1,128)S(1)} %bitcast.225), channel_id=1, replica_groups=mesh['ctx'=8,'fsdp'=16] {'fsdp'}, dimensions={0}, use_global_device_ids=true | all-gather | bytes 8704 | tf_op jit(solution)/shard_map/all_gather | solution.py:126
  114.6 2.2 reshape.337
  116.8 2.1 reshape.292
  118.9 2.7 fusion.46
  126.8 68.8 %all-gather.9.cloned.1.call-done = bf16[4,1024,8,128]{3,1,2,0:T(8,128)(2,1)} async-done(((bf16[4,128,8,128]{3,1,2,0:T(8,128)(2,1)}), bf16[4,1024,8,128]{3,1,2,0:T(8,128)(2,1)}) %all-gather.9.cloned.1.call-update) | async-done | bytes 8388624 | tf_op jit(solution)/shard_map/all_gather | solution.py:32
  195.6 10.4 %fusion.50 = (f32[2,8,2,128]{3,2,1,0:T(2,128)S(1)}, f32[2,8,2,128,1024]{3,4,2,1,0:T(8,128)}) fusion(bf16[2,128,8,2,128]{1,4,3,2,0:T(8,128)(2,1)S(1)} %fusion.18, bf16[4,1024,8,128]{3,1,2,0:T(8,128)(2,1)} %all-gather.9.cloned.1.call-done, pred[2,128,1024]{1,2,0:T(8,128)(4,1)} %broadcast_compare_fusion), kind=kOutput, calls=%fused_computation.141 | convolution fusion | flops 1086320640 | bytes 22298624 | tf_op jit(solution)/shard_map/sqkgd,stkd->skgqt/dot_general | solution.py:159
  206.0 8.4 fusion.3
  214.4 10.7 %fusion.22 = bf16[2,128,8,2,128]{1,4,3,2,0:T(8,128)(2,1)S(1)} fusion(f32[2,8,2,128,1024]{3,4,2,1,0:T(8,128)} %get-tuple-element.62, f32[2,8,2,128]{3,2,1,0:T(2,128)S(1)} %fusion.3, f32[2,8,2,128]{3,2,1,0:T(2,128)S(1)} %get-tuple-element.61, bf16[4,1024,8,128]{3,1,2,0:T(8,128)(2,1)} %all-gather.9.cloned.1.call-done), kind=kOutput, calls=%fused_computation.55 | convolution fusion | flops 1086849024 | bytes 22052864 | tf_op jit(solution)/shard_map/skgqt,stkd->sqkgd/dot_general | solution.py:170
  227.2 5.3 all-gather.11.cloned.1.call-done
  232.5 3.5 multiply_reduce_fusion.7
  236.3 70.3 %all-gather.13.cloned.1.call-done = bf16[1024,6144]{1,0:T(8,128)(2,1)} async-done(((bf16[64,6144]{1,0:T(8,128)(2,1)}), bf16[1024,6144]{1,0:T(8,128)(2,1)}) %all-gather.13.cloned.1.call-update) | async-done | bytes 12582928 | tf_op jit(solution)/shard_map/all_gather | solution.py:73
  306.5 6.4 fusion.51
  313.0 2.6 copy-done.3
  316.5 34.8 %all-gather.15.cloned.1.call-done = bf16[3072,1024]{1,0:T(8,128)(2,1)} async-done(((bf16[192,1024]{1,0:T(8,128)(2,1)}), bf16[3072,1024]{1,0:T(8,128)(2,1)}) %all-gather.15.cloned.1.call-update) | async-done | bytes 6291472 | tf_op jit(solution)/shard_map/all_gather | solution.py:73
  351.3 4.8 multiply_reduce_fusion.6
  357.9 4.2 multiply_convert_fusion.1
  362.1 7.8 multiply_reduce_fusion.3
  371.2 3.3 convolution_convert_fusion.3
  377.7 2.6 copy.157
  380.3 5.0 all-to-all-start.1
  385.3 11.9 %fusion = (f32[2,8,2,128]{3,2,1,0:T(2,128)S(1)}, f32[2,8,1024,128,2]{3,2,4,1,0:T(8,128)}) fusion(f32[2,8,2,128,1024]{3,4,2,1,0:T(8,128)} %get-tuple-element.62, f32[2,8,2,128]{3,2,1,0:T(2,128)S(1)} %bitcast.217, bf16[2,128,8,2,128]{1,4,3,2,0:T(8,128)(2,1)S(1)} %copy.157, bf16[4,1024,8,128]{3,1,2,0:T(8,128)(2,1)} %all-gather.9.cloned.1.call-done), kind=kOutput, calls=%fused_computation.2 | convolution fusion | flops 1086320640 | bytes 38830080 | tf_op jit(solution)/shard_map/sqkgd,stkd->skgqt/dot_general | solution.py:199
  397.3 11.8 %fusion.2 = bf16[2,8,2,128,1024]{3,4,2,1,0:T(8,128)(2,1)S(1)} fusion(f32[2,8,1024,128,2]{3,2,4,1,0:T(8,128)} %get-tuple-element.69, f32[2,8,2,128,1024]{3,4,2,1,0:T(8,128)} %get-tuple-element.62, f32[2,8,2,128]{3,2,1,0:T(2,128)S(1)} %get-tuple-element.68, f32[2,8,2,128]{3,2,1,0:T(2,128)S(1)} %bitcast.218), kind=kLoop, calls=%fused_computation.4 | loop fusion | flops 16777216 | bytes 41975808 | tf_op jit(solution)/shard_map/convert_element_type | solution.py:203
  409.1 3.2 copy-done
  412.3 4.3 fusion.10
  416.7 5.5 convolution_convert_fusion.2
  422.2 18.0 %all-to-all-done.1 = bf16[16,128,1024]{2,1,0:T(8,128)(2,1)} async-done(((bf16[16,128,1024]{2,1,0:T(8,128)(2,1)}), bf16[16,128,1024]{2,1,0:T(8,128)(2,1)}, u32[]{:S(2)}, u32[]{:S(2)}) %all-to-all-start.1) | async-done | bytes 4194336 | tf_op jit(solution)/shard_map/all_to_all | solution.py:22
  440.2 4.8 all-to-all-start.3
  445.0 8.0 convolution_convert_fusion
  453.0 87.1 %all-to-all-done.3 = bf16[16,192,1024]{2,1,0:T(8,128)(2,1)} async-done(((bf16[16,192,1024]{2,1,0:T(8,128)(2,1)}), bf16[16,192,1024]{2,1,0:T(8,128)(2,1)}, u32[]{:S(2)}, u32[]{:S(2)}) %all-to-all-start.3) | async-done | bytes 6291488 | tf_op jit(solution)/shard_map/all_to_all | solution.py:22
  540.1 4.9 all-to-all-start.2
  545.1 10.8 %fusion.11 = bf16[2,1024,8,128]{1,3,2,0:T(8,128)(2,1)} fusion(bf16[2,128,8,2,128]{1,4,3,2,0:T(8,128)(2,1)S(1)} %copy.157, f32[2,8,2,128,1024]{3,4,2,1,0:T(8,128)} %get-tuple-element.62, f32[2,8,2,128]{3,2,1,0:T(2,128)S(1)} %bitcast.219), kind=kOutput, calls=%fused_computation.22 | convolution fusion | flops 1084227584 | bytes 22036480 | tf_op jit(solution)/shard_map/skgqt,sqkgd->stkd/dot_general | solution.py:212
  555.9 7.1 copy.178
  563.0 6.2 copy.212
  570.2 6.2 fusion.20
  588.7 97.7 %reduce-scatter.7.cloned.1.call-done = bf16[128,2048]{1,0:T(8,128)(2,1)} async-done(((bf16[1024,2048]{1,0:T(8,128)(2,1)}), bf16[128,2048]{1,0:T(8,128)(2,1)}) %reduce-scatter.7.cloned.1.call-update) | async-done | bytes 524304
  691.6 7.7 convolution_convert_fusion.1
  699.3 14.0 %all-to-all-done.2 = bf16[16,64,6144]{2,1,0:T(8,128)(2,1)} async-done(((bf16[16,64,6144]{2,1,0:T(8,128)(2,1)}), bf16[16,64,6144]{2,1,0:T(8,128)(2,1)}, u32[]{:S(2)}, u32[]{:S(2)}) %all-to-all-start.2) | async-done | bytes 12582944 | tf_op jit(solution)/shard_map/all_to_all | solution.py:22
  713.4 4.8 all-to-all-start
  719.5 3.1 reduce_sum.185
  722.7 4.3 reduce_sum.187
  727.1 133.6 %all-reduce.7 = (bf16[2048]{0:T(1024)(128)(2,1)S(1)}, bf16[1024]{0:T(1024)(128)(2,1)S(1)}, bf16[1024]{0:T(1024)(128)(2,1)S(1)}, bf16[1024]{0:T(1024)(128)(2,1)S(1)}) all-reduce(f32[2048]{0:T(1024)S(1)} %get-tuple-element.13, f32[1024]{0:T(1024)S(1)} %get-tuple-element.15, ...), channel_id=4, replica_groups=mesh['ctx'=8,'fsdp'=16] {'fsdp'}, use_global_device_ids=true, to_apply=%region_18.19.clone | all-reduce | flops 5120 | bytes 30720
  861.0 6.9 reduce_sum.186
  868.1 5.0 reduce_sum.184
  873.2 21.0 %concatenate.63 = bf16[983360]{0:T(1024)(128)(2,1)} concatenate(bf16[262144]{0:T(1024)(128)(2,1)S(1)} %bitcast.203, bf16[131072]{0:T(1024)(128)(2,1)S(1)} %bitcast.211, bf16[393216]{0:T(1024)(128)(2,1)S(1)} %bitcast.200, bf16[196608]{0:T(1024)(128)(2,1)S(1)} %bitcast.209, bf16[128]{0:T(256)(128)(2,1)S(1)} %dynamic-slice.18, bf16[64]{0:T(256)(128)(2,1)S(1)} %dynamic-slice.17, ...), dimensions={0} | concatenate | bytes 3933440 | tf_op jit(solution)/shard_map/concatenate | solution.py:39
  894.2 7.2 fusion.23
  901.4 83.3 %all-reduce.11.cloned.1.call-done = bf16[983360]{0:T(1024)(128)(2,1)} async-done(((bf16[983360]{0:T(1024)(128)(2,1)}), bf16[983360]{0:T(1024)(128)(2,1)}) %all-reduce.11.cloned.1.call-update) | async-done | bytes 1966736 | tf_op jit(solution)/shard_map/psum | solution.py:39
  (195 shorter events, 73.7 us)
Async XLA Ops:
  7.2 65.8 %all-gather.7.cloned.1.call-start = ((), (), s32[]{:S(2)}) async-start(), calls=%async_computation.6 | async-start | bytes 8912896 | tf_op jit(solution)/shard_map/all_gather | solution.py:73
  9.2 186.5 %all-gather.9.cloned.1.call-start = ((), (), s32[]{:S(2)}) async-start(), calls=%async_computation.7 | async-start | bytes 9437184 | tf_op jit(solution)/shard_map/all_gather | solution.py:32
  71.6 9.3 copy-start.26
  78.8 2.2 copy-start.1
  80.9 1.7 copy-start.28
  87.6 5.4 copy-start.33
  87.6 5.6 copy-start.35
  88.7 143.7 %all-gather.11.cloned.1.call-start = ((), (), s32[]{:S(2)}) async-start(), calls=%async_computation.8 | async-start | bytes 4456448 | tf_op jit(solution)/shard_map/all_gather | solution.py:73
  89.5 217.1 %all-gather.13.cloned.1.call-start = ((), (), s32[]{:S(2)}) async-start(), calls=%async_computation.9 | async-start | bytes 13369344 | tf_op jit(solution)/shard_map/all_gather | solution.py:73
  91.6 259.7 %all-gather.15.cloned.1.call-start = ((), (), s32[]{:S(2)}) async-start(), calls=%async_computation.10 | async-start | bytes 6684672 | tf_op jit(solution)/shard_map/all_gather | solution.py:73
  109.1 7.7 copy-start.24
  112.6 4.2 copy-start.30
  121.7 3.2 copy-start.21
  126.8 79.2 %copy-start.6 = (bf16[2,128,8,2,128]{1,4,3,2,0:T(8,128)(2,1)}, bf16[2,128,8,2,128]{1,4,3,2,0:T(8,128)(2,1)S(1)}, u32[]{:S(2)}) copy-start(bf16[2,128,8,2,128]{1,4,3,2,0:T(8,128)(2,1)S(1)} %fusion.18) | copy-start | bytes 3145732
  227.2 8.9 copy-start.13
  236.0 70.5 %copy-start.8 = (f32[256,1024]{1,0:T(8,128)}, f32[256,1024]{1,0:T(8,128)S(1)}, u32[]{:S(2)}) copy-start(f32[256,1024]{1,0:T(8,128)S(1)} %get-tuple-element.64) | copy-start | bytes 3145732
  313.0 2.6 copy-start.3
  351.3 4.8 copy-start.11
  351.3 5.5 copy-start.4
  351.3 6.6 copy-start.36
  357.9 4.2 copy-start.10
  357.9 4.2 copy-start.9
  362.1 7.8 copy-start.14
  369.9 4.6 copy-start.18
  371.2 3.3 copy-start.37
  380.3 59.9 %all-to-all-start.1 = ((bf16[16,128,1024]{2,1,0:T(8,128)(2,1)}), bf16[16,128,1024]{2,1,0:T(8,128)(2,1)}, u32[]{:S(2)}, u32[]{:S(2)}) async-start(bf16[16,128,1024]{2,1,0:T(8,128)(2,1)} %bitcast.189), calls=%async_computation.2 | async-start | bytes 8388608 | tf_op jit(solution)/shard_map/all_to_all | solution.py:22
  385.3 199.4 %reduce-scatter.5.cloned.1.call-start = ((), (), s32[]{:S(2)}) async-start(), calls=%async_computation.11 | async-start | bytes 4718592 | tf_op jit(solution)/shard_map/reduce_scatter | solution.py:219
  397.3 15.1 %copy-start.7 = (bf16[2,128,8,2,128]{1,4,3,2,0:T(8,128)(2,1)S(1)}, bf16[2,128,8,2,128]{1,4,3,2,0:T(8,128)(2,1)}, u32[]{:S(2)}) copy-start(bf16[2,128,8,2,128]{1,4,3,2,0:T(8,128)(2,1)} %copy-done.6) | copy-start | bytes 3145732
  409.1 3.2 copy-start
  440.2 4.8 copy-start.16
  440.2 99.9 %all-to-all-start.3 = ((bf16[16,192,1024]{2,1,0:T(8,128)(2,1)}), bf16[16,192,1024]{2,1,0:T(8,128)(2,1)}, u32[]{:S(2)}, u32[]{:S(2)}) async-start(bf16[16,192,1024]{2,1,0:T(8,128)(2,1)} %bitcast.186), calls=%async_computation.4 | async-start | bytes 12582912 | tf_op jit(solution)/shard_map/all_to_all | solution.py:22
  540.1 173.3 %all-to-all-start.2 = ((bf16[16,64,6144]{2,1,0:T(8,128)(2,1)}), bf16[16,64,6144]{2,1,0:T(8,128)(2,1)}, u32[]{:S(2)}, u32[]{:S(2)}) async-start(bf16[16,64,6144]{2,1,0:T(8,128)(2,1)} %bitcast.185), calls=%async_computation.3 | async-start | bytes 25165824 | tf_op jit(solution)/shard_map/all_to_all | solution.py:22
  545.0 141.3 %reduce-scatter.7.cloned.1.call-start = ((), (), s32[]{:S(2)}) async-start(), calls=%async_computation.13 | async-start | bytes 4718592
  579.1 2.9 copy-start.2
  579.1 2.9 copy-start.25
  579.1 2.9 copy-start.31
  582.0 1.2 copy-start.34
  584.7 2.7 copy-start.5
  587.4 100.8 %copy-start.27 = (f32[1024]{0:T(1024)S(1)}, f32[1024]{0:T(1024)}, u32[]{:S(2)}) copy-start(f32[1024]{0:T(1024)} %copy-done.26) | copy-start | bytes 12292
  587.4 100.8 %copy-start.29 = (f32[256]{0:T(256)S(1)}, f32[256]{0:T(256)}, u32[]{:S(2)}) copy-start(f32[256]{0:T(256)} %copy-done.28) | copy-start | bytes 3076
  587.8 102.3 %copy-start.32 = (f32[256]{0:T(256)S(1)}, f32[256]{0:T(256)}, u32[]{:S(2)}) copy-start(f32[256]{0:T(256)} %get-tuple-element.53) | copy-start | bytes 3076
  588.6 102.9 %copy-start.15 = (bf16[2,128,1024]{2,1,0:T(8,128)(2,1)S(1)}, bf16[2,128,1024]{2,1,0:T(8,128)(2,1)}, u32[]{:S(2)}) copy-start(bf16[2,128,1024]{2,1,0:T(8,128)(2,1)} %param.14) | copy-start | bytes 1572868
  688.0 3.6 copy-start.20
  688.1 11.2 %copy-start.22 = (bf16[128,8,2,128]{3,1,2,0:T(8,128)(2,1)}, bf16[128,8,2,128]{3,1,2,0:T(8,128)(2,1)S(1)}, u32[]{:S(2)}) copy-start(bf16[128,8,2,128]{3,1,2,0:T(8,128)(2,1)S(1)} %copy.213) | copy-start | bytes 1572868
  691.6 7.8 copy-start.23
  713.4 154.7 %all-to-all-start = ((bf16[16,64,4096]{2,1,0:T(8,128)(2,1)}), bf16[16,64,4096]{2,1,0:T(8,128)(2,1)}, u32[]{:S(2)}, u32[]{:S(2)}) async-start(bf16[16,64,4096]{2,1,0:T(8,128)(2,1)} %bitcast.195), calls=%async_computation.1 | async-start | bytes 16777216 | tf_op jit(solution)/shard_map/all_to_all | solution.py:22
  718.2 266.6 %all-reduce.11.cloned.1.call-start = ((), (), s32[]{:S(2)}) async-start(), calls=%async_computation.12 | async-start | bytes 3936256 | tf_op jit(solution)/shard_map/psum | solution.py:39
  873.1 21.1 %copy-start.19 = (f32[256,1024]{1,0:T(8,128)S(1)}, f32[256,1024]{1,0:T(8,128)}, u32[]{:S(2)}) copy-start(f32[256,1024]{1,0:T(8,128)} %copy-done.18) | copy-start | bytes 3145732
  (2 other events, 1.9 us)
Sparse Core Ops, SparseCore 0:
  10.3 55.5 all-gather.6
  88.9 106.7 all-gather.8
  197.3 35.1 all-gather.10
  234.6 71.8 all-gather.12
  308.1 43.2 all-gather.14
  416.8 116.9 reduce-scatter.4
  569.4 116.9 reduce-scatter.6
  894.3 90.4 all-reduce.10
where the time goes:
time: 1010 us; the launch traced here: 1000 us
  waiting for transfers between devices  481 us (48%)
  blocking collectives  206 us (20%)
  matrix products  120 us (12%)
  local copies, waits for them, and re-layouts  82.6 us (8%)
  other arithmetic  77.5 us (8%)
  starting transfers between devices  19.8 us (2%)
  between operations  17.4 us (2%)
    unnamed x2, blocking collectives  191 us
    all_to_all x4, waiting for transfers between devices, sent_and_summed(): lax.all_to_all(pieces, axis, split_axis=0, concat_axis=0, tiled=True)  119 us
    all_gather x4, waiting for transfers between devices, fold_rows(): lax.all_gather(stacked, 'fsdp', axis=0, tiled=True)  110 us
    unnamed x9, waiting for transfers between devices  99 us
    psum x1, waiting for transfers between devices, packed_total(): so_far = lax.psum(jnp.concatenate([a.ravel() for a in arrays]), axis)  83.3 us
    all_gather x1, waiting for transfers between devices, sent_together(): lax.all_gather(both, axis, axis=dim, tiled=True)  68.8 us
    unnamed x97, local copies, waits for them, and re-layouts  29.3 us
    dot_general x4, matrix products, weight_grad(): lax.dot_general(left_rows, grad_rows, (((0,), (0,)), ((), ())), preferred...  24.5 us
  transfers between devices with their start and end apart: 12, of which 9 were waited for; matrix products, arithmetic and copies ran while one was open for 19% of the time, Pallas kernels for 0%

commit v1 on v0

v1 whole, which is shorter than its diff:
```python
import functools

import jax
import jax.numpy as jnp
from jax import lax
from jax.experimental import pallas as pl
from jax.experimental.pallas import tpu as pltpu
from jax.sharding import PartitionSpec as P

MESH = pl.DeviceIdType.MESH


def torus_place():
    at_ctx, at_fsdp = lax.axis_index("ctx"), lax.axis_index("fsdp")
    x = at_ctx // 4 * 2 + at_fsdp // 2 % 2
    return {"x": x, "y": at_fsdp // 4, "z": at_ctx % 4, "core": at_fsdp % 2}


def device_at(place):
    at_ctx = place["x"] // 2 * 4 + place["z"]
    at_fsdp = place["y"] * 4 + place["x"] % 2 * 2 + place["core"]
    return (at_ctx, at_fsdp)


def shifted(place, axis, by):
    return {**place, axis: (place[axis] + by) % 4}


def regions(place, axis, at, whole, columns, rows):
    here = {**place, axis: at}
    step = columns // 8
    row = pl.ds(rows[0], rows[1])
    ys = pl.ds(0, 4) if "y" in whole else pl.ds(here["y"], 1)
    los = pl.ds(0, 2) if "x" in whole else pl.ds(here["x"] % 2, 1)
    if "x" in whole and "z" in whole:
        return [(ys, los, row, pl.ds(0, columns))]
    if "z" in whole:
        return [(ys, los, row, pl.ds(pl.multiple_of(here["x"] // 2 * (4 * step), 128), 4 * step))]
    his = [0, 1] if "x" in whole else [here["x"] // 2]
    return [(ys, los, row, pl.ds(pl.multiple_of((hi * 4 + here["z"]) * step, 128), step)) for hi in his]


def greet(place, axes, sibling):
    barrier = pltpu.get_barrier_semaphore()
    others = [device_at(shifted(place, axis, by)) for axis in axes for by in (1, -1)]
    if sibling:
        others.append(device_at({**place, "core": 1 - place["core"]}))
    for other in others:
        pl.semaphore_signal(barrier, inc=1, device_id=other, device_id_type=MESH)
    pl.semaphore_wait(barrier, len(others))


class Copies:
    def __init__(self, send, recv):
        self.send, self.recv, self.used, self.sent = send, recv, 0, []

    def slot(self, count):
        first = self.used
        self.used += count
        return list(range(first, first + count))

    def make(self, slot, src, dst, device):
        return pltpu.make_async_remote_copy(
            src_ref=src, dst_ref=dst, send_sem=self.send.at[slot], recv_sem=self.recv.at[slot],
            device_id=device, device_id_type=MESH)

    def start(self, slot, src, dst, device):
        copy = self.make(slot, src, dst, device)
        copy.start()
        self.sent.append(copy)

    def finish(self):
        for copy in self.sent:
            copy.wait_send()
        self.sent = []


GATHER_ORDER = ("xyz", "yzx", "zxy")


def gather_kernel(part_of, gains, count, *refs):
    n = len(part_of)
    shards, gain_in = refs[:n], refs[n] if gains else None
    refs = refs[n + gains:]
    outs, gain_out = refs[:n], refs[n] if gains else None
    local_sem, send, recv = refs[n + gains:]
    place = torus_place()
    copies = Copies(send, recv)
    greet(place, "xyz", gains)
    mine = []
    for i, (shard, out) in enumerate(zip(shards, outs)):
        columns = out.shape[3]
        step = columns // 8
        at = pl.ds(pl.multiple_of((place["x"] // 2 * 4 + place["z"]) * step, 128), step)
        copy = pltpu.make_async_copy(shard.at[:, at], out.at[place["y"], place["x"] % 2, :, at], local_sem.at[i])
        copy.start()
        mine.append(copy)
    if gains:
        own_gain = pltpu.make_async_copy(gain_in, gain_out.at[place["y"], place["x"] % 2, place["core"]], local_sem.at[n])
        own_gain.start()
        own_gain.wait()
    for copy in mine:
        copy.wait()
    parts = [[i for i in range(n) if part_of[i] == part] for part in range(3)]

    def send_all(members, axis, at, whole, half, by, slots):
        slots = iter(slots)
        for i in members:
            out = outs[i]
            for where in regions(place, axis, at, whole, out.shape[3], half_rows(out, half)):
                copies.start(next(slots), out.at[where], out.at[where], device_at(shifted(place, axis, by)))

    def wait_all(members, axis, at, whole, half, by, slots):
        slots = iter(slots)
        for i in members:
            out = outs[i]
            for where in regions(place, axis, at, whole, out.shape[3], half_rows(out, half)):
                copies.make(next(slots), out.at[where], out.at[where], device_at(shifted(place, axis, by))).wait_recv()

    def half_rows(out, half):
        rows = out.shape[2]
        return (0, rows) if half is None else (half * (rows // 2), rows // 2)

    for phase in range(3):
        held = []
        for part in range(3):
            axis, whole = GATHER_ORDER[part][phase], GATHER_ORDER[part][:phase]
            members = parts[part]
            pieces = sum(len(regions(place, axis, place[axis], whole, outs[i].shape[3], (0, 16))) for i in members)
            slots = {(step, by): copies.slot(pieces) for step in (0, 1) for by in (1, -1)}
            held.append((members, axis, whole, slots))
            for by in (1, -1):
                send_all(members, axis, place[axis], whole, None, by, slots[0, by])
        if gains and phase == 0:
            gain_slots = {(step, by): copies.slot(1)[0] for step in (0, 1) for by in (1, -1)}
            for by in (1, -1):
                where = gain_out.at[place["y"], place["x"] % 2, place["core"]]
                copies.start(gain_slots[0, by], where, where, device_at(shifted(place, "y", by)))
        for members, axis, whole, slots in held:
            for by in (1, -1):
                behind = (place[axis] - by) % 4
                wait_all(members, axis, behind, whole, None, -by, slots[0, by])
                send_all(members, axis, behind, whole, 0 if by == 1 else 1, by, slots[1, by])
        if gains and phase == 0:
            for by in (1, -1):
                behind = (place["y"] - by) % 4
                where = gain_out.at[behind, place["x"] % 2, place["core"]]
                copies.make(gain_slots[0, by], where, where, device_at(shifted(place, "y", -by))).wait_recv()
            behind = (place["y"] - 1) % 4
            where = gain_out.at[behind, place["x"] % 2, place["core"]]
            copies.start(gain_slots[1, 1], where, where, device_at(shifted(place, "y", 1)))
        for members, axis, whole, slots in held:
            for by in (1, -1):
                wait_all(members, axis, (place[axis] + 2) % 4, whole, 0 if by == 1 else 1, -by, slots[1, by])
        if gains and phase == 0:
            where = gain_out.at[(place["y"] + 2) % 4, place["x"] % 2, place["core"]]
            copies.make(gain_slots[1, 1], where, where, device_at(shifted(place, "y", -1))).wait_recv()
        if gains and phase == 1:
            other = {**place, "x": place["x"] // 2 * 2 + (1 - place["x"] % 2)}
            slot = copies.slot(1)[0]
            where = gain_out.at[:, place["x"] % 2, place["core"]]
            copies.start(slot, where, where, device_at(other))
            where = gain_out.at[:, 1 - place["x"] % 2, place["core"]]
            copies.make(slot, where, where, device_at(other)).wait_recv()
    copies.finish()
    if gains:
        other = device_at({**place, "core": 1 - place["core"]})
        slot = copies.slot(1)[0]
        where = gain_out.at[:, :, place["core"]]
        copies.start(slot, where, where, other)
        where = gain_out.at[:, :, 1 - place["core"]]
        copies.make(slot, where, where, other).wait_recv()
        copies.finish()
    assert copies.used <= count, copies.used


def gather_weights(shards, part_of, gain_tile, collective_id, count):
    gains = gain_tile is not None
    outs = [jax.ShapeDtypeStruct((4, 2) + s.shape, s.dtype) for s in shards]
    operands = list(shards)
    if gains:
        outs.append(jax.ShapeDtypeStruct((4, 2, 2) + gain_tile.shape, gain_tile.dtype))
        operands.append(gain_tile)
    return pl.pallas_call(
        functools.partial(gather_kernel, part_of, gains, count),
        out_shape=outs,
        in_specs=[pl.BlockSpec(memory_space=pl.ANY)] * len(operands),
        out_specs=[pl.BlockSpec(memory_space=pl.ANY)] * len(outs),
        scratch_shapes=[pltpu.SemaphoreType.DMA((len(operands),)), pltpu.SemaphoreType.DMA((count,)), pltpu.SemaphoreType.DMA((count,))],
        compiler_params=pltpu.CompilerParams(collective_id=collective_id, has_side_effects=True),
        name="gather_weights",
    )(*operands)


def add_region(acc, temp, at, extra=()):
    ys, los, rows, columns = at
    chunk = 32
    per = rows.size // chunk

    def one(step, carry):
        del carry
        row = step % per * chunk
        lo = step // per % los.size
        y = step // (per * los.size)

        def view(ref, where):
            r = pl.ds(pl.multiple_of(where[2].start + row, 16), chunk)
            return ref.at[where[0].start + y, where[1].start + lo, r, where[3]]

        total = view(acc, at)[...].astype(jnp.float32)
        for t in extra:
            total += view(temp, t)[...].astype(jnp.float32)
        view(acc, at)[...] = total.astype(jnp.bfloat16)
        return 0

    lax.fori_loop(0, per * los.size * ys.size, one, 0)


def reduce_kernel(part_of, count, *refs):
    n = len(part_of)
    grads, outs = refs[:n], refs[n:2 * n]
    accs, temps = refs[2 * n:3 * n], refs[3 * n:4 * n]
    local_sem, send, recv = refs[4 * n:]
    place = torus_place()
    copies = Copies(send, recv)
    loads = []
    for i in range(n):
        load = pltpu.make_async_copy(grads[i], accs[i], local_sem.at[i])
        load.start()
        loads.append(load)
    barrier = pltpu.get_barrier_semaphore()
    far = device_at(shifted(place, "x", 2))
    others = [device_at(shifted(place, axis, by)) for axis in "xyz" for by in (1, -1)] + [far]
    for other in others:
        pl.semaphore_signal(barrier, inc=1, device_id=other, device_id_type=MESH)
    pl.semaphore_wait(barrier, len(others))
    parts = [[i for i in range(n) if part_of[i] == part] for part in range(3)]

    def half_rows(i, half):
        rows = accs[i].shape[2]
        return (half * (rows // 2), rows // 2)

    def blocks(i, phase, part, at, half, landing):
        order = GATHER_ORDER[part]
        here = place
        if landing:
            for axis in order[phase + 1:]:
                here = shifted(here, axis, 1 if half else -1)
        return regions(here, order[phase], at % 4, order[:phase], accs[i].shape[3], half_rows(i, half))

    def send_block(phase, part, at, half, by, land_at, slots):
        slots = iter(slots)
        device = device_at(shifted(place, GATHER_ORDER[part][phase], by))
        for i in parts[part]:
            for src, dst in zip(blocks(i, phase, part, at, half, False), blocks(i, phase, part, land_at, half, True)):
                copies.start(next(slots), accs[i].at[src], temps[i].at[dst], device)

    def wait_block(phase, part, half, by, land_at, slots):
        slots = iter(slots)
        device = device_at(shifted(place, GATHER_ORDER[part][phase], -by))
        for i in parts[part]:
            for dst in blocks(i, phase, part, land_at, half, True):
                copies.make(next(slots), temps[i].at[dst], temps[i].at[dst], device).wait_recv()

    def add_block(phase, part, at, half, land_ats):
        for i in parts[part]:
            where = blocks(i, phase, part, at, half, False)
            landed = [blocks(i, phase, part, land_at, half, True) for land_at in land_ats]
            for k, region in enumerate(where):
                add_region(accs[i], temps[i], region, [t[k] for t in landed])

    for phase in (2, 1, 0):
        slots = {}
        for part in range(3):
            c = place[GATHER_ORDER[part][phase]]
            pieces = sum(len(blocks(i, phase, part, c, 0, False)) for i in parts[part])
            if phase == 2:
                for i in parts[part]:
                    loads[i].wait()
            for by in (1, -1):
                half = 0 if by == 1 else 1
                slots[part, by] = [copies.slot(pieces) for _ in range(3)]
                send_block(phase, part, c + 2, half, by, c + 2, slots[part, by][0])
            for by in (1, -1):
                half = 0 if by == 1 else 1
                send_block(phase, part, c + by, 1 - half, by, c + by if by == 1 else c + 1, slots[part, by][1])
        for part in range(3):
            c = place[GATHER_ORDER[part][phase]]
            for by in (1, -1):
                half = 0 if by == 1 else 1
                wait_block(phase, part, half, by, c + by, slots[part, by][0])
                add_block(phase, part, c + by, half, [c + by])
                send_block(phase, part, c + by, half, by, c + by if by == 1 else c + 1, slots[part, by][2])
        for part in range(3):
            c = place[GATHER_ORDER[part][phase]]
            for half in (0, 1):
                for by in (1, -1):
                    first = half == (0 if by == 1 else 1)
                    wait_block(phase, part, half, by, c if by == 1 else c + 2, slots[part, by][2 if first else 1])
                add_block(phase, part, c, half, [c, c + 2])
    finish_kernel(part_of, accs, outs, place, copies, local_sem)
    assert copies.used <= count, copies.used


def finish_kernel(part_of, accs, outs, place, copies, local_sem):
    n = len(part_of)

    def block(i, x, z):
        step = outs[i].shape[1] // 8
        return outs[i].at[:, pl.ds(pl.multiple_of(((x % 4) // 2 * 4 + z % 4) * step, 128), step)]

    def halves(i, x, z, half):
        step = outs[i].shape[1] // 8
        rows = outs[i].shape[0] // 2
        return outs[i].at[pl.ds(half * rows, rows), pl.ds(pl.multiple_of(((x % 4) // 2 * 4 + z % 4) * step, 128), step)]

    x, z = place["x"], place["z"]
    stores = []
    for i in range(n):
        step = outs[i].shape[1] // 8
        at = pl.ds(pl.multiple_of((x // 2 * 4 + z) * step, 128), step)
        store = pltpu.make_async_copy(accs[i].at[place["y"], x % 2, :, at], block(i, x, z), local_sem.at[i])
        store.start()
        stores.append(store)
    for store in stores:
        store.wait()
    far = device_at(shifted(place, "x", 2))
    up, down = device_at(shifted(place, "z", 1)), device_at(shifted(place, "z", -1))
    slots = {name: copies.slot(n) for name in ("far", "up", "down", "far_up", "far_down", "two_up", "two_down", "far_two_up", "far_two_down")}

    def send(name, view, device):
        for i in range(n):
            copies.start(slots[name][i], view(i), view(i), device)

    def wait(name, view, device):
        for i in range(n):
            copies.make(slots[name][i], view(i), view(i), device).wait_recv()

    send("far", lambda i: block(i, x, z), far)
    send("up", lambda i: block(i, x, z), up)
    send("down", lambda i: block(i, x, z), down)
    wait("far", lambda i: block(i, x + 2, z), far)
    send("far_up", lambda i: block(i, x + 2, z), up)
    send("far_down", lambda i: block(i, x + 2, z), down)
    wait("up", lambda i: block(i, x, z - 1), down)
    send("two_up", lambda i: halves(i, x, z - 1, 0), up)
    wait("down", lambda i: block(i, x, z + 1), up)
    send("two_down", lambda i: halves(i, x, z + 1, 1), down)
    wait("far_up", lambda i: block(i, x + 2, z - 1), down)
    send("far_two_up", lambda i: halves(i, x + 2, z - 1, 0), up)
    wait("far_down", lambda i: block(i, x + 2, z + 1), up)
    send("far_two_down", lambda i: halves(i, x + 2, z + 1, 1), down)
    wait("two_up", lambda i: halves(i, x, z + 2, 0), down)
    wait("two_down", lambda i: halves(i, x, z + 2, 1), up)
    wait("far_two_up", lambda i: halves(i, x + 2, z + 2, 0), down)
    wait("far_two_down", lambda i: halves(i, x + 2, z + 2, 1), up)
    copies.finish()


def reduce_grads(grads, part_of, collective_id, count):
    shapes = [g.shape for g in grads]
    return pl.pallas_call(
        functools.partial(reduce_kernel, part_of, count),
        out_shape=[jax.ShapeDtypeStruct(s[2:], jnp.bfloat16) for s in shapes],
        in_specs=[pl.BlockSpec(memory_space=pl.ANY)] * len(grads),
        out_specs=[pl.BlockSpec(memory_space=pl.ANY)] * len(grads),
        scratch_shapes=[pltpu.VMEM(s, jnp.bfloat16) for s in shapes] * 2
        + [pltpu.SemaphoreType.DMA((len(grads),)), pltpu.SemaphoreType.DMA((count,)), pltpu.SemaphoreType.DMA((count,))],
        compiler_params=pltpu.CompilerParams(collective_id=collective_id, has_side_effects=True, vmem_limit_bytes=50 << 20),
        name="reduce_grads",
    )(*grads)


HEAD = 128
SPAN = 64
TILE = 256
score_scale = HEAD ** (-0.5)


def dot(a, b, a_dim, b_dim):
    return lax.dot_general(a, b, (((a_dim,), (b_dim,)), ((), ())), preferred_element_type=jnp.float32)


def gather_sorted(order_ref, seq, ref, column, width, out, out_at):
    for j in range(16):
        slot = order_ref[seq, j]
        rows = ref[slot // 2, 0, pl.ds(slot % 2 * SPAN, SPAN), column:column + width]
        out[out_at + j * SPAN:out_at + (j + 1) * SPAN, :] = rows


def tile_scores(q, k, low, high):
    scores = dot(q, k, 1, 1) * score_scale
    rows = lax.broadcasted_iota(jnp.int32, scores.shape, 0) % TILE + low
    keys = lax.broadcasted_iota(jnp.int32, scores.shape, 1)
    return jnp.where(keys <= rows, scores, -1e30)


def forward_kernel(order_ref, qkv_ref, out_ref, lse_ref, q_s, k_s, v_s):
    seq = pl.program_id(0)
    gather_sorted(order_ref, seq, qkv_ref, 0, HEAD, q_s.at[0], 0)
    gather_sorted(order_ref, seq, qkv_ref, HEAD, HEAD, q_s.at[1], 0)
    gather_sorted(order_ref, seq, qkv_ref, 2 * HEAD, HEAD, k_s, 0)
    gather_sorted(order_ref, seq, qkv_ref, 3 * HEAD, HEAD, v_s, 0)
    for i in range(1024 // TILE):
        low, high = i * TILE, (i + 1) * TILE
        q = q_s[:, low:high, :].reshape(2 * TILE, HEAD)
        scores = tile_scores(q, k_s[:high], low, high)
        top = jnp.max(scores, -1, keepdims=True)
        raised = jnp.exp(scores - top)
        total = jnp.sum(raised, -1, keepdims=True)
        probs = (raised * (1.0 / total)).astype(jnp.bfloat16)
        out = dot(probs, v_s[:high], 1, 0).astype(jnp.bfloat16)
        lse_ref[0, :, low:high, :] = jnp.broadcast_to(top + jnp.log(total), (2 * TILE, HEAD)).reshape(2, TILE, HEAD)
        for j in range(TILE // SPAN):
            slot = order_ref[seq, low // SPAN + j]
            for h in range(2):
                out_ref[slot // 2, 0, pl.ds(slot % 2 * SPAN, SPAN), h * HEAD:(h + 1) * HEAD] = out[
                    h * TILE + j * SPAN:h * TILE + (j + 1) * SPAN]


def attention_forward(order, qkv):
    return pl.pallas_call(
        forward_kernel,
        grid_spec=pltpu.PrefetchScalarGridSpec(
            num_scalar_prefetch=1, grid=(2,),
            in_specs=[pl.BlockSpec((8, 1, 128, 4 * HEAD), lambda s, order: (0, s, 0, 0))],
            out_specs=[pl.BlockSpec((8, 1, 128, 2 * HEAD), lambda s, order: (0, s, 0, 0)),
                       pl.BlockSpec((1, 2, 1024, HEAD), lambda s, order: (s, 0, 0, 0))],
            scratch_shapes=[pltpu.VMEM((2, 1024, HEAD), jnp.bfloat16), pltpu.VMEM((1024, HEAD), jnp.bfloat16), pltpu.VMEM((1024, HEAD), jnp.bfloat16)]),
        out_shape=[jax.ShapeDtypeStruct((8, 2, 128, 2 * HEAD), jnp.bfloat16), jax.ShapeDtypeStruct((2, 2, 1024, HEAD), jnp.float32)],
        compiler_params=pltpu.CompilerParams(vmem_limit_bytes=40 << 20),
        cost_estimate=pl.CostEstimate(flops=1400000000, bytes_accessed=6 << 20, transcendentals=3 << 20),
        name="attention_forward",
    )(order, qkv)


def backward_kernel(order_ref, qkv_ref, grad_ref, lse_ref, out_ref, q_s, k_s, v_s, g_s, dk_s, dv_s):
    seq = pl.program_id(0)
    gather_sorted(order_ref, seq, qkv_ref, 0, HEAD, q_s.at[0], 0)
    gather_sorted(order_ref, seq, qkv_ref, HEAD, HEAD, q_s.at[1], 0)
    gather_sorted(order_ref, seq, qkv_ref, 2 * HEAD, HEAD, k_s, 0)
    gather_sorted(order_ref, seq, qkv_ref, 3 * HEAD, HEAD, v_s, 0)
    gather_sorted(order_ref, seq, grad_ref, 0, HEAD, g_s.at[0], 0)
    gather_sorted(order_ref, seq, grad_ref, HEAD, HEAD, g_s.at[1], 0)
    tiles = 1024 // TILE
    for i in reversed(range(tiles)):
        low, high = i * TILE, (i + 1) * TILE
        q = q_s[:, low:high, :].reshape(2 * TILE, HEAD)
        g = g_s[:, low:high, :].reshape(2 * TILE, HEAD)
        k, v = k_s[:high], v_s[:high]
        lse = lse_ref[0, :, low:high, :].reshape(2 * TILE, HEAD)[:, :1]
        probs = jnp.exp(tile_scores(q, k, low, high) - lse)
        grad_probs = dot(g, v, 1, 1)
        inner = jnp.sum(probs * grad_probs, -1, keepdims=True)
        grad_scores = (probs * (grad_probs - inner)).astype(jnp.bfloat16)
        probs_low = probs.astype(jnp.bfloat16)
        dq = (dot(grad_scores, k, 1, 0) * score_scale).astype(jnp.bfloat16)
        dk = dot(grad_scores, q, 0, 0)
        dv = dot(probs_low, g, 0, 0)
        if i == tiles - 1:
            dk_s[...] = dk
            dv_s[...] = dv
        else:
            dk_s[:high] += dk
            dv_s[:high] += dv
        for j in range(TILE // SPAN):
            slot = order_ref[seq, low // SPAN + j]
            for h in range(2):
                out_ref[slot // 2, 0, pl.ds(slot % 2 * SPAN, SPAN), h * HEAD:(h + 1) * HEAD] = dq[
                    h * TILE + j * SPAN:h * TILE + (j + 1) * SPAN]
    for j in range(16):
        slot = order_ref[seq, j]
        rows = pl.ds(slot % 2 * SPAN, SPAN)
        at = slice(j * SPAN, (j + 1) * SPAN)
        out_ref[slot // 2, 0, rows, 2 * HEAD:3 * HEAD] = (dk_s[at] * score_scale).astype(jnp.bfloat16)
        out_ref[slot // 2, 0, rows, 3 * HEAD:] = dv_s[at].astype(jnp.bfloat16)


def attention_backward(order, qkv, grad, lse):
    return pl.pallas_call(
        backward_kernel,
        grid_spec=pltpu.PrefetchScalarGridSpec(
            num_scalar_prefetch=1, grid=(2,),
            in_specs=[pl.BlockSpec((8, 1, 128, 4 * HEAD), lambda s, order: (0, s, 0, 0)),
                      pl.BlockSpec((8, 1, 128, 2 * HEAD), lambda s, order: (0, s, 0, 0)),
                      pl.BlockSpec((1, 2, 1024, HEAD), lambda s, order: (s, 0, 0, 0))],
            out_specs=pl.BlockSpec((8, 1, 128, 4 * HEAD), lambda s, order: (0, s, 0, 0)),
            scratch_shapes=[pltpu.VMEM((2, 1024, HEAD), jnp.bfloat16), pltpu.VMEM((1024, HEAD), jnp.bfloat16), pltpu.VMEM((1024, HEAD), jnp.bfloat16),
                            pltpu.VMEM((2, 1024, HEAD), jnp.bfloat16), pltpu.VMEM((1024, HEAD), jnp.float32), pltpu.VMEM((1024, HEAD), jnp.float32)]),
        out_shape=jax.ShapeDtypeStruct((8, 2, 128, 4 * HEAD), jnp.bfloat16),
        compiler_params=pltpu.CompilerParams(vmem_limit_bytes=40 << 20),
        cost_estimate=pl.CostEstimate(flops=3400000000, bytes_accessed=8 << 20, transcendentals=3 << 20),
        name="attention_backward",
    )(order, qkv, grad, lse)


HEADS = 16
KV_HEADS = 8
rope_base = 1000000.0
norm_eps = 1e-06
PART = (1, 2, 2, 0, 0, 1, 2)


def rms_forward(values, norm_gain):
    inverse = lax.rsqrt(jnp.mean(values * values, -1, keepdims=True) + norm_eps)
    return (values * inverse * norm_gain, inverse)


def rms_backward(values, inverse, norm_gain, upstream):
    scaled = upstream * norm_gain
    row_inner = jnp.mean(scaled * values, -1, keepdims=True)
    grad_values = inverse * scaled - values * (inverse * inverse * inverse) * row_inner
    grad_gain = jnp.sum(upstream * values * inverse, 0)
    return (grad_values, grad_gain)


def angles(positions):
    steps_half = jnp.arange(HEAD // 2, dtype=jnp.float32)
    inverse_freq = rope_base ** (-2.0 * steps_half / HEAD)
    phase = positions.astype(jnp.float32)[..., None] * inverse_freq
    phase = jnp.concatenate([phase, phase], -1)
    return (jnp.cos(phase), jnp.sin(phase))


def rotate(values, cosine, sine):
    half_width = values.shape[-1] // 2
    turned = jnp.concatenate([-values[..., half_width:], values[..., :half_width]], -1)
    return values * cosine + turned * sine


def to_sibling(array):
    return lax.ppermute(array, "fsdp", [(i, i ^ 1) for i in range(16)])


def split_columns(rows, core):
    count, width = rows.shape
    stripe = width // 16
    both = rows.reshape(count, 8, 2, stripe).transpose(2, 0, 1, 3).reshape(2, count, width // 2)
    return (lax.dynamic_index_in_dim(both, core, 0, keepdims=False), lax.dynamic_index_in_dim(both, 1 - core, 0, keepdims=False))


def join_columns(own, sibling, core):
    count, half = own.shape
    even = jnp.where(core == 0, own, sibling)
    odd = jnp.where(core == 0, sibling, own)
    both = jnp.stack([even.reshape(count, 8, half // 8), odd.reshape(count, 8, half // 8)], 2)
    return both.reshape(count, 2 * half)


def fold_rows(parts, weights):
    return dot(parts[0], weights[0], 1, 0) + dot(parts[1], weights[1], 1, 0)


def fold_back(grad_rows, weights):
    return [dot(grad_rows, w, 1, 1) for w in weights]


def weight_grad(parts, grad_rows):
    from_sibling = to_sibling(dot(parts[1], grad_rows, 0, 0).astype(jnp.bfloat16))
    total = (dot(parts[0], grad_rows, 0, 0) + from_sibling.astype(jnp.float32)).astype(jnp.bfloat16)
    return total.reshape(4, 2, total.shape[0] // 8, total.shape[1])


def per_device(
    tokens,
    span_order,
    w_query,
    w_key,
    w_value,
    w_out,
    w_gate,
    w_up,
    w_down,
    query_gain,
    key_gain,
    attn_gain,
    ffn_gain,
    cotangent,
):
    seq_local, rows_local, width = tokens.shape
    span_rows = rows_local // 2
    total_rows = seq_local * rows_local
    query_width = HEADS * HEAD
    key_width = KV_HEADS * HEAD
    core = lax.axis_index("fsdp") % 2
    ctx_index = lax.axis_index("ctx")
    token_rows = tokens.reshape(total_rows, width)

    gains_here = jnp.concatenate([query_gain, key_gain, attn_gain, ffn_gain, jnp.zeros((704,), jnp.float32)])
    *gathered, gains_all = gather_weights(
        (w_query, w_key, w_value, w_out, w_gate, w_up, w_down), PART, gains_here.reshape(8, 128), 1, 200)
    own_weights = [w.reshape(8 * w.shape[2], w.shape[3]) for w in gathered]
    pairs = [(w, to_sibling(w)) for w in own_weights]
    wq, wk, wv, wo, wg, wu, wd = pairs
    gains_all = gains_all.reshape(16, 1024)
    q_gain_all = gains_all[:, :128].reshape(-1)
    k_gain_all = gains_all[:, 128:192].reshape(-1)
    a_gain_all = gains_all[:, 192:256].reshape(-1)
    f_gain_all = gains_all[:, 256:320].reshape(-1)

    own_spans = lax.dynamic_slice_in_dim(span_order, 2 * ctx_index, 2, 1)
    offsets = jnp.arange(span_rows, dtype=jnp.int32)
    query_pos = (own_spans[:, :, None] * span_rows + offsets).reshape(seq_local, rows_local)
    cosine, sine = angles(query_pos)
    cosine = cosine[:, :, None, :]
    sine = sine[:, :, None, :]
    numbers = jnp.arange(16, dtype=jnp.int32)
    slot_of = jnp.sum(jnp.where(span_order[:, :, None] == numbers, numbers[None, :, None], 0), 1)

    token_parts = split_columns(token_rows, core)
    query_raw = fold_rows(token_parts, wq)
    key_raw = fold_rows(token_parts, wk)
    value_raw = fold_rows(token_parts, wv)
    query_normed, query_inverse = rms_forward(query_raw, q_gain_all)
    key_normed, key_inverse = rms_forward(key_raw, k_gain_all)
    query_rot = rotate(query_normed.reshape(seq_local, rows_local, HEADS, HEAD), cosine, sine)
    key_rot = rotate(key_normed.reshape(seq_local, rows_local, KV_HEADS, HEAD), cosine, sine)

    def by_heads(array, heads):
        array = array.astype(jnp.bfloat16).reshape(seq_local, rows_local, KV_HEADS, heads * HEAD)
        return array.transpose(2, 0, 1, 3)

    def by_rows(array):
        return array.transpose(1, 2, 0, 3).reshape(total_rows, -1)

    sent = jnp.concatenate([by_heads(query_rot, 2), by_heads(key_rot, 1), by_heads(value_raw, 1)], -1)
    qkv = lax.all_to_all(sent, "ctx", split_axis=0, concat_axis=0, tiled=True)
    out_heads, lse = attention_forward(slot_of, qkv)
    attended = lax.all_to_all(out_heads, "ctx", split_axis=0, concat_axis=0, tiled=True)
    attended_low = by_rows(attended)
    attended_parts = split_columns(attended_low, core)
    branch = fold_rows(attended_parts, wo)
    branch_normed, branch_inverse = rms_forward(branch, a_gain_all)
    mixed = token_rows.astype(jnp.float32) + branch_normed
    mixed_low = mixed.astype(jnp.bfloat16)
    mixed_parts = split_columns(mixed_low, core)
    gate = fold_rows(mixed_parts, wg)
    upward = fold_rows(mixed_parts, wu)
    middle_low = (jax.nn.silu(gate) * upward).astype(jnp.bfloat16)
    middle_parts = split_columns(middle_low, core)
    ffn_out = fold_rows(middle_parts, wd)
    ffn_normed, ffn_inverse = rms_forward(ffn_out, f_gain_all)
    layer_out = (mixed + ffn_normed).astype(jnp.bfloat16).reshape(seq_local, rows_local, width)

    grad_rows_out = cotangent.reshape(total_rows, width).astype(jnp.float32)
    grad_ffn, grad_ffn_gain = rms_backward(ffn_out, ffn_inverse, f_gain_all, grad_rows_out)
    grad_ffn_low = grad_ffn.astype(jnp.bfloat16)
    grad_middle = join_columns(*fold_back(grad_ffn_low, wd), core)
    sigmoid_gate = jax.nn.sigmoid(gate)
    grad_gate = (grad_middle * upward * sigmoid_gate * (1.0 + gate * (1.0 - sigmoid_gate))).astype(jnp.bfloat16)
    grad_upward = (grad_middle * jax.nn.silu(gate)).astype(jnp.bfloat16)
    from_gate = fold_back(grad_gate, wg)
    from_up = fold_back(grad_upward, wu)
    grad_mixed = grad_rows_out + join_columns(from_gate[0] + from_up[0], from_gate[1] + from_up[1], core)
    grad_branch, grad_attn_gain = rms_backward(branch, branch_inverse, a_gain_all, grad_mixed)
    grad_branch_low = grad_branch.astype(jnp.bfloat16)
    grad_attended = join_columns(*fold_back(grad_branch_low, wo), core).astype(jnp.bfloat16)
    grad_sent = grad_attended.reshape(seq_local, rows_local, KV_HEADS, 2 * HEAD).transpose(2, 0, 1, 3)
    grad_heads = lax.all_to_all(grad_sent, "ctx", split_axis=0, concat_axis=0, tiled=True)
    grad_qkv_heads = attention_backward(slot_of, qkv, grad_heads, lse)
    grad_qkv = lax.all_to_all(grad_qkv_heads, "ctx", split_axis=0, concat_axis=0, tiled=True)
    shard_down = weight_grad(middle_parts, grad_ffn_low)
    shard_gate = weight_grad(mixed_parts, grad_gate)
    shard_up = weight_grad(mixed_parts, grad_upward)
    shard_out = weight_grad(attended_parts, grad_branch_low)

    def rows_of(first, heads):
        return grad_qkv[..., first * HEAD : (first + heads) * HEAD].transpose(1, 2, 0, 3).astype(jnp.float32)

    grad_query_rot = rotate(rows_of(0, 2).reshape(seq_local, rows_local, HEADS, HEAD), cosine, -sine)
    grad_query_raw, grad_query_gain = rms_backward(
        query_raw, query_inverse, q_gain_all, grad_query_rot.reshape(total_rows, query_width))
    grad_key_rot = rotate(rows_of(2, 1), cosine, -sine)
    grad_key_raw, grad_key_gain = rms_backward(
        key_raw, key_inverse, k_gain_all, grad_key_rot.reshape(total_rows, key_width))
    grad_query_low = grad_query_raw.astype(jnp.bfloat16)
    grad_key_low = grad_key_raw.astype(jnp.bfloat16)
    grad_value_low = rows_of(3, 1).reshape(total_rows, key_width).astype(jnp.bfloat16)
    shard_query = weight_grad(token_parts, grad_query_low)
    shard_key = weight_grad(token_parts, grad_key_low)
    shard_value = weight_grad(token_parts, grad_value_low)
    from_query = fold_back(grad_query_low, wq)
    from_key = fold_back(grad_key_low, wk)
    from_value = fold_back(grad_value_low, wv)
    grad_tokens = grad_mixed + join_columns(*(a + b + c for a, b, c in zip(from_query, from_key, from_value)), core)
    grad_tokens = grad_tokens.astype(jnp.bfloat16).reshape(seq_local, rows_local, width)
    gain_totals = lax.psum(jnp.concatenate([grad_query_gain, grad_key_gain, grad_attn_gain, grad_ffn_gain]), ("ctx", "fsdp"))
    at = lax.axis_index("fsdp")

    def own_gain(first, count):
        return lax.dynamic_slice_in_dim(gain_totals, first + at * count, count)

    totals = reduce_grads(
        (shard_query, shard_key, shard_value, shard_out, shard_gate, shard_up, shard_down), PART, 2, 400)
    return (
        layer_out,
        grad_tokens,
        *(total.astype(jnp.float32) for total in totals),
        own_gain(0, 128),
        own_gain(2048, 64),
        own_gain(3072, 64),
        own_gain(4096, 64),
    )


def solution(mesh):
    rows, shard, gain = P("fsdp", "ctx", None), P("fsdp", None), P("fsdp")
    return jax.shard_map(
        per_device,
        mesh=mesh,
        in_specs=(rows, shard) + (shard,) * 7 + (gain,) * 4 + (rows,),
        out_specs=(rows, rows) + (shard,) * 7 + (gain,) * 4,
        check_vma=False,
    )
```

time: 1010 us -> 613 us (0.61)
  waiting for transfers between devices: 481 us -> 63.3 us
  Pallas kernels: 0 us -> 203 us
  blocking collectives: 206 us -> 65.4 us
  other arithmetic: 77.5 us -> 52.9 us
  matrix products: 120 us -> 98.8 us
  local copies, waits for them, and re-layouts: 82.6 us -> 99.9 us
  between operations: 17.4 us -> 2.21 us
    pallas_call x0 -> x4, Pallas kernels: none -> 203 us  [the longest x1 97.6 us: reduce_grads(): pl.pallas_call(functools.partial(reduce_kernel, part_of, count), out_shap...]
    unnamed x2 -> x0, blocking collectives: 191 us -> none
    all_gather x5 -> x0, waiting for transfers between devices: 179 us -> none  [the longest x4 110 us: fold_rows(): lax.all_gather(stacked, 'fsdp', axis=0, tiled=True)]
    unnamed x9 -> x0, waiting for transfers between devices: 99 us -> none
    psum x1 -> x0, waiting for transfers between devices: 83.3 us -> none  [packed_total(): so_far = lax.psum(jnp.concatenate([a.ravel() for a in arrays]), axis)]
    psum x0 -> x1, blocking collectives: none -> 65.4 us  [per_device(): lax.psum(jnp.concatenate([grad_query_gain, grad_key_gain, grad_attn_gain,...]
    all_to_all x4, waiting for transfers between devices: 119 us -> 63.3 us  [the longest x1 25.6 us: per_device(): qkv = lax.all_to_all(sent, 'ctx', split_axis=0, concat_axis=0, tiled=True)]
    reduce_sum x7 -> x1, other arithmetic: 29.8 us -> 0.09 us  [per_device(): jnp.sum(jnp.where(span_order[:, :, None] == numbers, numbers[None, :, Non...]
  transfers between devices with their start and end apart: 12 -> 18, of which waited for: 9 -> 4; matrix products, arithmetic and copies ran while one was open for 19% -> 24% of each run, Pallas kernels for 0% -> 3%
where the time goes in v1:
time: 613 us; the launch traced here: 608 us
  Pallas kernels  203 us (33%)
  local copies, waits for them, and re-layouts  99.9 us (16%)
  matrix products  98.8 us (16%)
  blocking collectives  65.4 us (11%)
  waiting for transfers between devices  63.3 us (10%)
  other arithmetic  52.9 us (9%)
  starting transfers between devices  22.8 us (4%)
    dot_general x42, matrix products, dot(): lax.dot_general(a, b, (((a_dim,), (b_dim,)), ((), ())), preferred_element...  98.8 us
    pallas_call x1, Pallas kernels, reduce_grads(): pl.pallas_call(functools.partial(reduce_kernel, part_of, count), out_shap...  97.6 us
    pallas_call x1, Pallas kernels, gather_weights(): pl.pallas_call(functools.partial(gather_kernel, part_of, gains, count), o...  85.4 us
    psum x1, blocking collectives, per_device(): lax.psum(jnp.concatenate([grad_query_gain, grad_key_gain, grad_attn_gain,...  65.4 us
    unnamed x171, local copies, waits for them, and re-layouts  27.8 us
    all_to_all x1, waiting for transfers between devices, per_device(): qkv = lax.all_to_all(sent, 'ctx', split_axis=0, concat_axis=0, tiled=True)  25.6 us
    all_to_all x1, waiting for transfers between devices, per_device(): lax.all_to_all(out_heads, 'ctx', split_axis=0, concat_axis=0, tiled=True)  12.7 us
    all_to_all x1, waiting for transfers between devices, per_device(): lax.all_to_all(grad_sent, 'ctx', split_axis=0, concat_axis=0, tiled=True)  12.5 us
  transfers between devices with their start and end apart: 18, of which 4 were waited for; matrix products, arithmetic and copies ran while one was open for 24% of the time, Pallas kernels for 3%

profile of v1, /device:TPU:0, one launch (start us, length us, event | category | flops | bytes accessed | tf_op | source)
XLA Modules:
  0.0 608.2 jit_solution(5214086172637721687)
XLA Ops:
  2.1 85.4 %gather_weights.1 = (bf16[4,2,64,2048]{3,2,1,0:T(8,128)(2,1)}, bf16[4,2,64,1024]{3,2,1,0:T(8,128)(2,1)}, bf16[4,2,64,1024]{3,2,1,0:T(8,128)(2,1)}, bf16[4,2,128,...) custom-call(bf16[64,2048]{1,0:T(8,128)(2,1)} %refs_0_.1, ...), custom_call_target="tpu_custom_call" | custom-call | tf_op jit(solution)/shard_map/gather_weights/pallas_call | solution.py:184
  91.3 2.9 fusion.83
  96.1 3.8 fusion.85
  103.6 2.9 copy.81
  127.4 2.8 maximum_multiply_fusion
  130.1 3.0 copy.85
  133.2 3.1 fusion.6
  137.9 4.9 all-to-all-start
  143.8 25.6 %all-to-all-done.qkv_ref = bf16[8,2,128,512]{3,2,1,0:T(8,128)(2,1)S(1)} async-done(((bf16[8,2,128,512]{3,2,1,0:T(8,128)(2,1)}), bf16[8,2,128,512]{3,2,1,0:T(8,128)(2,1)S(1)}, u32[]{:S(2)}, u32[]{:S(2)}) %all-to-all-start) | async-done | bytes 2097184 | tf_op jit(solution)/shard_map/all_to_all | solution.py:627
  169.5 8.9 %attention_forward.1 = (bf16[8,2,128,256]{3,2,1,0:T(8,128)(2,1)}, f32[2,2,1024,128]{3,2,1,0:T(8,128)S(1)}) custom-call(s32[2,16]{1,0:T(2,128)S(1)} %select_reduce_fusion.order_ref, bf16[8,2,128,512]{3,2,1,0:T(8,128)(2,1)S(1)} %all-to-all-done.qkv_ref), custom_call_target="tpu_custom_call" | custom-call | flops 1400000000 | bytes 6291456 | tf_op jit(solution)/shard_map/attention_forward/pallas_call | solution.py:422
  179.7 4.9 all-to-all-start.1
  187.9 12.7 %all-to-all-done.1 = bf16[8,2,128,256]{3,2,1,0:T(8,128)(2,1)} async-done(((bf16[8,2,128,256]{3,2,1,0:T(8,128)(2,1)}), bf16[8,2,128,256]{3,2,1,0:T(8,128)(2,1)}, u32[]{:S(2)}, u32[]{:S(2)}) %all-to-all-start.1) | async-done | bytes 1048608 | tf_op jit(solution)/shard_map/all_to_all | solution.py:629
  202.7 3.7 copy.90
  216.6 3.1 fusion.62
  220.8 3.0 convolution_add_fusion.1
  223.9 6.9 %multiply_convert_fusion.2 = (bf16[256,3072]{1,0:T(8,128)(2,1)}, f32[256,3072]{1,0:T(8,128)}) fusion(f32[256,3072]{1,0:T(8,128)S(1)} %convolution_add_fusion.1, f32[256,3072]{1,0:T(8,128)S(1)} %fusion.62, bf16[512,3072]{1,0:T(8,128)(2,1)} %collective-permute-done.5, bf16[2,256,512]{1,2,0:T(8,128)(2,1)S(1)} %bitcast.332, s32[]{:T(128)S(6)} %select_n.88), kind=kOutput, calls=%fused_computation.13 | convolution fusion | flops 810811392 | bytes 14417924 | tf_op jit(solution)/shard_map/dot_general | solution.py:381
  230.8 2.6 copy.93
  236.8 3.0 multiply_reduce_fusion.7
  242.1 4.7 broadcast_select_fusion.1
  246.8 3.0 copy.97
  249.8 3.0 copy.98
  257.1 3.8 copy.100
  260.9 4.7 multiply_convert_fusion.1
  269.8 3.1 fusion.148
  272.9 4.0 broadcast_select_fusion.5
  285.9 2.6 multiply_reduce_fusion.3
  299.9 4.7 all-to-all-start.2
  304.5 3.3 convolution_convert_fusion.4
  307.9 12.5 %all-to-all-done.2.grad_ref = bf16[8,2,128,256]{3,2,1,0:T(8,128)(2,1)S(1)} async-done(((bf16[8,2,128,256]{3,2,1,0:T(8,128)(2,1)}), bf16[8,2,128,256]{3,2,1,0:T(8,128)(2,1)S(1)}, u32[]{:S(2)}, u32[]{:S(2)}) %all-to-all-start.2) | async-done | bytes 1048608 | tf_op jit(solution)/shard_map/all_to_all | solution.py:659
  322.0 10.9 %attention_backward.1 = bf16[8,2,128,512]{3,2,1,0:T(8,128)(2,1)S(1)} custom-call(s32[2,16]{1,0:T(2,128)S(1)} %select_reduce_fusion.order_ref, bf16[8,2,128,512]{3,2,1,0:T(8,128)(2,1)S(1)} %all-to-all-done.qkv_ref, bf16[8,2,128,256]{3,2,1,0:T(8,128)(2,1)S(1)} %all-to-all-done.2.grad_ref, f32[2,2,1024,128]{3,2,1,0:T(8,128)S(1)} %copy-done.2), custom_call_target="tpu_custom_call" | custom-call | flops 3400000000 | bytes 8388608 | tf_op jit(solution)/shard_map/attention_backward/pallas_call | solution.py:480
  334.2 4.5 all-to-all-start.3
  340.4 2.8 convolution_convert_fusion.2
  343.2 2.6 convolution_convert_fusion
  346.3 2.8 convolution_convert_fusion.1
  349.1 3.7 add_convert_fusion.3
  352.9 12.4 %all-to-all-done.3 = bf16[8,2,128,512]{3,2,1,0:T(8,128)(2,1)} async-done(((bf16[8,2,128,512]{3,2,1,0:T(8,128)(2,1)}), bf16[8,2,128,512]{3,2,1,0:T(8,128)(2,1)}, u32[]{:S(2)}, u32[]{:S(2)}) %all-to-all-start.3) | async-done | bytes 2097184 | tf_op jit(solution)/shard_map/all_to_all | solution.py:661
  365.3 2.7 convert_bitcast_fusion
  368.0 3.1 copy.111
  371.1 4.2 copy.109
  383.2 3.0 copy.113
  408.1 2.7 reshape.319
  410.8 65.4 %psum.7 = f32[5120]{0:T(1024)S(1)} all-reduce(f32[5120]{0:T(1024)S(1)} %pad_maximum_fusion.6), channel_id=1, replica_groups=mesh['ctx'=8,'fsdp'=16] {'ctx','fsdp'}, use_global_device_ids=true, to_apply=%region_13.14 | all-reduce | flops 5120 | bytes 40960 | tf_op jit(solution)/shard_map/psum | solution.py:687
  477.4 3.1 add_convert_fusion.7
  484.0 4.5 add_convert_fusion.1
  488.6 4.7 add_convert_fusion
  493.3 4.6 add_convert_fusion.2
  500.7 3.6 add_convert_fusion.4
  504.4 97.6 %reduce_grads.1 = (bf16[64,2048]{1,0:T(8,128)(2,1)S(1)}, bf16[64,1024]{1,0:T(8,128)(2,1)S(1)}, bf16[64,1024]{1,0:T(8,128)(2,1)S(1)}, bf16[128,1024]{1,0:T(8,128)...) custom-call(bf16[4,2,64,2048]{3,2,1,0:T(8,128)(2,1)} %bitcast.352, ...), custom_call_target="tpu_custom_call" | custom-call | tf_op jit(solution)/shard_map/reduce_grads/pallas_call | solution.py:362
  (311 shorter events, 134.1 us)
Async XLA Ops:
  0.6 88.1 %copy-start.46 = (bf16[2,128,1024]{2,1,0:T(8,128)(2,1)S(1)}, bf16[2,128,1024]{2,1,0:T(8,128)(2,1)}, u32[]{:S(2)}) copy-start(bf16[2,128,1024]{2,1,0:T(8,128)(2,1)} %param.14) | copy-start | bytes 1572868
  87.5 27.4 %collective-permute-start = (bf16[512,2048]{1,0:T(8,128)(2,1)}, bf16[512,2048]{1,0:T(8,128)(2,1)S(1)}, u32[]{:S(2)}, u32[]{:S(2)}) collective-permute-start(bf16[512,2048]{1,0:T(8,128)(2,1)} %bitcast.382), channel_id=1, source_target_pairs={{0,1},{1,0},{2,3},{3,2},{4,5},{5,4},{6,7},{7,6},{8,9},{9,8},{10,11... | collective-permute-start | bytes 6291464 | tf_op jit(solution)/shard_map/ppermute | solution.py:532
  88.0 18.6 %collective-permute-start.1 = (bf16[512,1024]{1,0:T(8,128)(2,1)}, bf16[512,1024]{1,0:T(8,128)(2,1)}, u32[]{:S(2)}, u32[]{:S(2)}) collective-permute-start(bf16[512,1024]{1,0:T(8,128)(2,1)} %bitcast.367), channel_id=1, source_target_pairs={{0,1},{1,0},{2,3},{3,2},{4,5},{5,4},{6,7},{7,6},{8,9},{9,8},{10,11... | collective-permute-start | bytes 3145736 | tf_op jit(solution)/shard_map/ppermute | solution.py:532
  88.1 21.9 %collective-permute-start.2 = (bf16[512,1024]{1,0:T(8,128)(2,1)}, bf16[512,1024]{1,0:T(8,128)(2,1)}, u32[]{:S(2)}, u32[]{:S(2)}) collective-permute-start(bf16[512,1024]{1,0:T(8,128)(2,1)} %bitcast.364), channel_id=1, source_target_pairs={{0,1},{1,0},{2,3},{3,2},{4,5},{5,4},{6,7},{7,6},{8,9},{9,8},{10,11... | collective-permute-start | bytes 3145736 | tf_op jit(solution)/shard_map/ppermute | solution.py:532
  91.3 23.7 %copy-start.5 = (bf16[2,256,8,64]{1,3,2,0:T(8,128)(2,1)}, bf16[2,256,8,64]{1,3,2,0:T(8,128)(2,1)S(1)}, u32[]{:S(2)}) copy-start(bf16[2,256,8,64]{1,3,2,0:T(8,128)(2,1)S(1)} %copy.78) | copy-start | bytes 1572868
  91.3 4.4 copy-start.66
  91.3 4.4 copy-start.77
  137.9 31.6 %all-to-all-start = ((bf16[8,2,128,512]{3,2,1,0:T(8,128)(2,1)}), bf16[8,2,128,512]{3,2,1,0:T(8,128)(2,1)S(1)}, u32[]{:S(2)}, u32[]{:S(2)}) async-start(bf16[8,2,128,512]{3,2,1,0:T(8,128)(2,1)} %pad_maximum_fusion.1), calls=%async_computation | async-start | bytes 4194304 | tf_op jit(solution)/shard_map/all_to_all | solution.py:627
  142.7 66.3 %collective-permute-start.3 = (bf16[1024,1024]{1,0:T(8,128)(2,1)}, bf16[1024,1024]{1,0:T(8,128)(2,1)}, u32[]{:S(2)}, u32[]{:S(2)}) collective-permute-start(bf16[1024,1024]{1,0:T(8,128)(2,1)} %bitcast.385), channel_id=1, source_target_pairs={{0,1},{1,0},{2,3},{3,2},{4,5},{5,4},{6,7},{7,6},{8,9},{9,8},{10,11... | collective-permute-start | bytes 6291464 | tf_op jit(solution)/shard_map/ppermute | solution.py:532
  142.8 78.1 %collective-permute-start.4 = (bf16[512,3072]{1,0:T(8,128)(2,1)}, bf16[512,3072]{1,0:T(8,128)(2,1)}, u32[]{:S(2)}, u32[]{:S(2)}) collective-permute-start(bf16[512,3072]{1,0:T(8,128)(2,1)} %bitcast.377), channel_id=1, source_target_pairs={{0,1},{1,0},{2,3},{3,2},{4,5},{5,4},{6,7},{7,6},{8,9},{9,8},{10,11... | collective-permute-start | bytes 9437192 | tf_op jit(solution)/shard_map/ppermute | solution.py:532
  179.7 5.6 copy-start.68
  179.7 5.6 copy-start.67
  179.7 5.7 copy-start.65
  179.7 20.9 %all-to-all-start.1 = ((bf16[8,2,128,256]{3,2,1,0:T(8,128)(2,1)}), bf16[8,2,128,256]{3,2,1,0:T(8,128)(2,1)}, u32[]{:S(2)}, u32[]{:S(2)}) async-start(bf16[8,2,128,256]{3,2,1,0:T(8,128)(2,1)} %get-tuple-element.34), calls=%async_computation.1 | async-start | bytes 2097152 | tf_op jit(solution)/shard_map/all_to_all | solution.py:629
  184.6 39.3 %collective-permute-start.5 = (bf16[512,3072]{1,0:T(8,128)(2,1)}, bf16[512,3072]{1,0:T(8,128)(2,1)}, u32[]{:S(2)}, u32[]{:S(2)}) collective-permute-start(bf16[512,3072]{1,0:T(8,128)(2,1)} %bitcast.374), channel_id=1, source_target_pairs={{0,1},{1,0},{2,3},{3,2},{4,5},{5,4},{6,7},{7,6},{8,9},{9,8},{10,11... | collective-permute-start | bytes 9437192 | tf_op jit(solution)/shard_map/ppermute | solution.py:532
  184.6 52.2 %collective-permute-start.6 = (bf16[1536,1024]{1,0:T(8,128)(2,1)}, bf16[1536,1024]{1,0:T(8,128)(2,1)}, u32[]{:S(2)}, u32[]{:S(2)}) collective-permute-start(bf16[1536,1024]{1,0:T(8,128)(2,1)} %bitcast.371), channel_id=1, source_target_pairs={{0,1},{1,0},{2,3},{3,2},{4,5},{5,4},{6,7},{7,6},{8,9},{9,8},{10,11... | collective-permute-start | bytes 9437192 | tf_op jit(solution)/shard_map/ppermute | solution.py:532
  209.0 3.5 copy-start.47
  216.6 7.2 %copy-start.28 = (bf16[2,256,8,64]{1,3,2,0:T(8,128)(2,1)}, bf16[2,256,8,64]{1,3,2,0:T(8,128)(2,1)S(1)}, u32[]{:S(2)}) copy-start(bf16[2,256,8,64]{1,3,2,0:T(8,128)(2,1)S(1)} %copy.92) | copy-start | bytes 1572868
  216.6 3.2 copy-start.57
  223.8 6.9 %copy-start.27 = (f32[256,3072]{1,0:T(8,128)}, f32[256,3072]{1,0:T(8,128)S(1)}, u32[]{:S(2)}) copy-start(f32[256,3072]{1,0:T(8,128)S(1)} %convolution_add_fusion.1) | copy-start | bytes 9437188
  260.9 4.8 copy-start.58
  265.7 4.1 copy-start.17
  265.7 7.2 %copy-start.7 = (bf16[256,3072]{1,0:T(8,128)(2,1)}, bf16[256,3072]{1,0:T(8,128)(2,1)S(1)}, u32[]{:S(2)}) copy-start(bf16[256,3072]{1,0:T(8,128)(2,1)S(1)} %get-tuple-element.82) | copy-start | bytes 4718596
  291.1 3.2 copy-start.49
  299.9 20.5 %all-to-all-start.2 = ((bf16[8,2,128,256]{3,2,1,0:T(8,128)(2,1)}), bf16[8,2,128,256]{3,2,1,0:T(8,128)(2,1)S(1)}, u32[]{:S(2)}, u32[]{:S(2)}) async-start(bf16[8,2,128,256]{3,2,1,0:T(8,128)(2,1)} %bitcast.370), calls=%async_computation.2 | async-start | bytes 2097152 | tf_op jit(solution)/shard_map/all_to_all | solution.py:659
  307.9 41.3 %collective-permute-start.10 = (bf16[1024,1024]{1,0:T(8,128)(2,1)}, bf16[1024,1024]{1,0:T(8,128)(2,1)}, u32[]{:S(2)}, u32[]{:S(2)}) collective-permute-start(bf16[1024,1024]{1,0:T(8,128)(2,1)} %convolution_convert_fusion.4), channel_id=1, source_target_pairs={{0,1},{1,0},{2,3},{3,2},{4,5},{5,4},{6,7},{7,6},{8,9},{9,8},{10,11... | collective-permute-start | bytes 6291464 | tf_op jit(solution)/shard_map/ppermute | solution.py:532
  334.2 4.6 copy-start.36
  334.2 31.1 %all-to-all-start.3 = ((bf16[8,2,128,512]{3,2,1,0:T(8,128)(2,1)}), bf16[8,2,128,512]{3,2,1,0:T(8,128)(2,1)}, u32[]{:S(2)}, u32[]{:S(2)}) async-start(bf16[8,2,128,512]{3,2,1,0:T(8,128)(2,1)} %copy-done), calls=%async_computation.3 | async-start | bytes 4194304 | tf_op jit(solution)/shard_map/all_to_all | solution.py:661
  343.2 3.1 copy-start.8
  343.2 145.3 %collective-permute-start.13 = (bf16[1536,1024]{1,0:T(8,128)(2,1)}, bf16[1536,1024]{1,0:T(8,128)(2,1)}, u32[]{:S(2)}, u32[]{:S(2)}) collective-permute-start(bf16[1536,1024]{1,0:T(8,128)(2,1)} %convolution_convert_fusion.2), channel_id=1, source_target_pairs={{0,1},{1,0},{2,3},{3,2},{4,5},{5,4},{6,7},{7,6},{8,9},{9,8},{10,11... | collective-permute-start | bytes 9437192 | tf_op jit(solution)/shard_map/ppermute | solution.py:532
  345.8 3.3 copy-start.39
  345.8 3.3 copy-start.50
  345.8 137.2 %collective-permute-start.12 = (bf16[512,3072]{1,0:T(8,128)(2,1)}, bf16[512,3072]{1,0:T(8,128)(2,1)}, u32[]{:S(2)}, u32[]{:S(2)}) collective-permute-start(bf16[512,3072]{1,0:T(8,128)(2,1)} %convolution_convert_fusion), channel_id=1, source_target_pairs={{0,1},{1,0},{2,3},{3,2},{4,5},{5,4},{6,7},{7,6},{8,9},{9,8},{10,11... | collective-permute-start | bytes 9437192 | tf_op jit(solution)/shard_map/ppermute | solution.py:532
  349.1 144.2 %collective-permute-start.11 = (bf16[512,3072]{1,0:T(8,128)(2,1)}, bf16[512,3072]{1,0:T(8,128)(2,1)}, u32[]{:S(2)}, u32[]{:S(2)}) collective-permute-start(bf16[512,3072]{1,0:T(8,128)(2,1)} %convolution_convert_fusion.1), channel_id=1, source_target_pairs={{0,1},{1,0},{2,3},{3,2},{4,5},{5,4},{6,7},{7,6},{8,9},{9,8},{10,11... | collective-permute-start | bytes 9437192 | tf_op jit(solution)/shard_map/ppermute | solution.py:532
  389.2 13.5 %copy-start.23 = (bf16[2,128,8,128]{3,2,1,0:T(8,128)(2,1)}, bf16[2,128,8,128]{3,2,1,0:T(8,128)(2,1)S(1)}, u32[]{:S(2)}) copy-start(bf16[2,128,8,128]{3,2,1,0:T(8,128)(2,1)S(1)} %copy.115) | copy-start | bytes 1572868
  390.7 107.2 %collective-permute-start.9 = (bf16[512,1024]{1,0:T(8,128)(2,1)}, bf16[512,1024]{1,0:T(8,128)(2,1)}, u32[]{:S(2)}, u32[]{:S(2)}) collective-permute-start(bf16[512,1024]{1,0:T(8,128)(2,1)} %convolution_convert_fusion.5), channel_id=1, source_target_pairs={{0,1},{1,0},{2,3},{3,2},{4,5},{5,4},{6,7},{7,6},{8,9},{9,8},{10,11... | collective-permute-start | bytes 3145736 | tf_op jit(solution)/shard_map/ppermute | solution.py:532
  394.5 8.7 %copy-start.15 = (bf16[256,2048]{1,0:T(8,128)(2,1)}, bf16[256,2048]{1,0:T(8,128)(2,1)S(1)}, u32[]{:S(2)}) copy-start(bf16[256,2048]{1,0:T(8,128)(2,1)S(1)} %subtract_convert_fusion) | copy-start | bytes 3145732
  396.7 103.3 %collective-permute-start.7 = (bf16[512,2048]{1,0:T(8,128)(2,1)}, bf16[512,2048]{1,0:T(8,128)(2,1)}, u32[]{:S(2)}, u32[]{:S(2)}) collective-permute-start(bf16[512,2048]{1,0:T(8,128)(2,1)} %convolution_convert_fusion.3), channel_id=1, source_target_pairs={{0,1},{1,0},{2,3},{3,2},{4,5},{5,4},{6,7},{7,6},{8,9},{9,8},{10,11... | collective-permute-start | bytes 6291464 | tf_op jit(solution)/shard_map/ppermute | solution.py:532
  397.3 4.5 copy-start.25
  397.3 3.7 copy-start.60
  407.0 3.9 copy-start.74
  407.0 3.9 copy-start.75
  407.0 70.4 %copy-start.48 = (bf16[2,128,1024]{1,0,2:T(2,128)(2,1)S(1)}, bf16[2,128,1024]{1,0,2:T(2,128)(2,1)}, u32[]{:S(2)}) copy-start(bf16[2,128,1024]{1,0,2:T(2,128)(2,1)} %copy.95) | copy-start | bytes 1572868
  477.4 5.2 copy-start.26
  483.0 5.5 copy-start.22
  483.1 5.5 copy-start.33
  483.1 16.5 %collective-permute-start.8 = (bf16[512,1024]{1,0:T(8,128)(2,1)S(1)}, bf16[512,1024]{1,0:T(8,128)(2,1)S(1)}, u32[]{:S(2)}, u32[]{:S(2)}) collective-permute-start(bf16[512,1024]{1,0:T(8,128)(2,1)S(1)} %convolution_convert_fusion.6), channel_id=1, source_target_pairs={{0,1},{1,0},{2,3},{3,2},{4,5},{5,4},{6,7},{7,6},{8,9},{9,8},{10,11... | collective-permute-start | bytes 3145736 | tf_op jit(solution)/shard_map/ppermute | solution.py:532
  493.3 4.6 copy-start.24
  (49 other events, 99.0 us)

commit v2 on v1

v2 whole, which is shorter than its diff:
```python
import functools

import jax
import jax.numpy as jnp
from jax import lax
from jax.experimental import pallas as pl
from jax.experimental.pallas import tpu as pltpu
from jax.sharding import PartitionSpec as P

MESH = pl.DeviceIdType.MESH


def torus_place():
    at_ctx, at_fsdp = lax.axis_index("ctx"), lax.axis_index("fsdp")
    x = at_ctx // 4 * 2 + at_fsdp // 2 % 2
    return {"x": x, "y": at_fsdp // 4, "z": at_ctx % 4, "core": at_fsdp % 2}


def device_at(place):
    at_ctx = place["x"] // 2 * 4 + place["z"]
    at_fsdp = place["y"] * 4 + place["x"] % 2 * 2 + place["core"]
    return (at_ctx, at_fsdp)


def shifted(place, axis, by):
    return {**place, axis: (place[axis] + by) % 4}


def regions(place, axis, at, whole, columns, rows, first=0):
    here = {**place, axis: at}
    step = columns // 8
    row = pl.ds(rows[0], rows[1])
    ys = pl.ds(0, 4) if "y" in whole else pl.ds(here["y"], 1)
    los = pl.ds(0, 2) if "x" in whole else pl.ds(here["x"] % 2, 1)
    if "x" in whole and "z" in whole:
        return [(ys, los, row, pl.ds(first, columns))]
    if "z" in whole:
        return [(ys, los, row, pl.ds(pl.multiple_of(first + here["x"] // 2 * (4 * step), 128), 4 * step))]
    his = [0, 1] if "x" in whole else [here["x"] // 2]
    return [(ys, los, row, pl.ds(pl.multiple_of(first + (hi * 4 + here["z"]) * step, 128), step)) for hi in his]


def greet(place, axes, sibling):
    barrier = pltpu.get_barrier_semaphore()
    others = [device_at(shifted(place, axis, by)) for axis in axes for by in (1, -1)]
    if sibling:
        others.append(device_at({**place, "core": 1 - place["core"]}))
    for other in others:
        pl.semaphore_signal(barrier, inc=1, device_id=other, device_id_type=MESH)
    pl.semaphore_wait(barrier, len(others))


class Copies:
    def __init__(self, send, recv):
        self.send, self.recv, self.used, self.sent = send, recv, 0, []

    def slot(self, count):
        first = self.used
        self.used += count
        return list(range(first, first + count))

    def make(self, slot, src, dst, device):
        return pltpu.make_async_remote_copy(
            src_ref=src, dst_ref=dst, send_sem=self.send.at[slot], recv_sem=self.recv.at[slot],
            device_id=device, device_id_type=MESH)

    def start(self, slot, src, dst, device):
        copy = self.make(slot, src, dst, device)
        copy.start()
        self.sent.append(copy)

    def finish(self):
        for copy in self.sent:
            copy.wait_send()
        self.sent = []


GATHER_ORDER = ("xyz", "yzx", "zxy")


def gather_kernel(members, gains, count, *refs):
    n, n_out = len(members), 1 + max(m[1] for m in members)
    shards, gain_in = refs[:n], refs[n] if gains else None
    refs = refs[n + gains:]
    outs, gain_out = refs[:n_out], refs[n_out] if gains else None
    local_sem, send, recv = refs[n_out + gains:]
    place = torus_place()
    copies = Copies(send, recv)
    greet(place, "xyz", gains)
    mine = []
    for i, (_, o, first) in enumerate(members):
        step = shards[i].shape[1] // 8
        at = (place["x"] // 2 * 4 + place["z"]) * step
        copy = pltpu.make_async_copy(
            shards[i].at[:, pl.ds(pl.multiple_of(at, 128), step)],
            outs[o].at[place["y"], place["x"] % 2, :, pl.ds(pl.multiple_of(first + at, 128), step)], local_sem.at[i])
        copy.start()
        mine.append(copy)
    if gains:
        own_gain = pltpu.make_async_copy(gain_in, gain_out.at[place["y"], place["x"] % 2, place["core"]], local_sem.at[n])
        own_gain.start()
        own_gain.wait()
    for copy in mine:
        copy.wait()
    parts = [[i for i in range(n) if members[i][0] == part] for part in range(3)]

    def views(group, axis, at, whole, half):
        for i in group:
            _, o, first = members[i]
            rows = shards[i].shape[0]
            rows = (0, rows) if half is None else (half * (rows // 2), rows // 2)
            for where in regions(place, axis, at, whole, shards[i].shape[1], rows, first):
                yield outs[o].at[where]

    def send_all(group, axis, at, whole, half, by, slots):
        for slot, view in zip(slots, views(group, axis, at, whole, half), strict=True):
            copies.start(slot, view, view, device_at(shifted(place, axis, by)))

    def wait_all(group, axis, at, whole, half, by, slots):
        for slot, view in zip(slots, views(group, axis, at, whole, half), strict=True):
            copies.make(slot, view, view, device_at(shifted(place, axis, by))).wait_recv()

    for phase in range(3):
        held = []
        for part in range(3):
            axis, whole = GATHER_ORDER[part][phase], GATHER_ORDER[part][:phase]
            pieces = len(list(views(parts[part], axis, place[axis], whole, None)))
            slots = {(step, by): copies.slot(pieces) for step in (0, 1) for by in (1, -1)}
            held.append((parts[part], axis, whole, slots))
            for by in (1, -1):
                send_all(parts[part], axis, place[axis], whole, None, by, slots[0, by])
        if gains and phase == 0:
            gain_slots = {(step, by): copies.slot(1)[0] for step in (0, 1) for by in (1, -1)}
            for by in (1, -1):
                where = gain_out.at[place["y"], place["x"] % 2, place["core"]]
                copies.start(gain_slots[0, by], where, where, device_at(shifted(place, "y", by)))
        for group, axis, whole, slots in held:
            for by in (1, -1):
                behind = (place[axis] - by) % 4
                wait_all(group, axis, behind, whole, None, -by, slots[0, by])
                send_all(group, axis, behind, whole, 0 if by == 1 else 1, by, slots[1, by])
        if gains and phase == 0:
            for by in (1, -1):
                behind = (place["y"] - by) % 4
                where = gain_out.at[behind, place["x"] % 2, place["core"]]
                copies.make(gain_slots[0, by], where, where, device_at(shifted(place, "y", -by))).wait_recv()
            behind = (place["y"] - 1) % 4
            where = gain_out.at[behind, place["x"] % 2, place["core"]]
            copies.start(gain_slots[1, 1], where, where, device_at(shifted(place, "y", 1)))
        for group, axis, whole, slots in held:
            for by in (1, -1):
                wait_all(group, axis, (place[axis] + 2) % 4, whole, 0 if by == 1 else 1, -by, slots[1, by])
        if gains and phase == 0:
            where = gain_out.at[(place["y"] + 2) % 4, place["x"] % 2, place["core"]]
            copies.make(gain_slots[1, 1], where, where, device_at(shifted(place, "y", -1))).wait_recv()
        if gains and phase == 1:
            other = {**place, "x": place["x"] // 2 * 2 + (1 - place["x"] % 2)}
            slot = copies.slot(1)[0]
            where = gain_out.at[:, place["x"] % 2, place["core"]]
            copies.start(slot, where, where, device_at(other))
            where = gain_out.at[:, 1 - place["x"] % 2, place["core"]]
            copies.make(slot, where, where, device_at(other)).wait_recv()
    copies.finish()
    if gains:
        other = device_at({**place, "core": 1 - place["core"]})
        slot = copies.slot(1)[0]
        where = gain_out.at[:, :, place["core"]]
        copies.start(slot, where, where, other)
        where = gain_out.at[:, :, 1 - place["core"]]
        copies.make(slot, where, where, other).wait_recv()
        copies.finish()
    assert copies.used <= count, copies.used


def gather_weights(shards, members, gain_tile, collective_id, count):
    gains = gain_tile is not None
    widths = [0] * (1 + max(m[1] for m in members))
    rows = list(widths)
    for shard, (_, o, first) in zip(shards, members):
        rows[o], widths[o] = shard.shape[0], max(widths[o], first + shard.shape[1])
    outs = [jax.ShapeDtypeStruct((4, 2, r, w), jnp.bfloat16) for r, w in zip(rows, widths)]
    operands = list(shards)
    if gains:
        outs.append(jax.ShapeDtypeStruct((4, 2, 2) + gain_tile.shape, gain_tile.dtype))
        operands.append(gain_tile)
    return pl.pallas_call(
        functools.partial(gather_kernel, members, gains, count),
        out_shape=outs,
        in_specs=[pl.BlockSpec(memory_space=pl.ANY)] * len(operands),
        out_specs=[pl.BlockSpec(memory_space=pl.ANY)] * len(outs),
        scratch_shapes=[pltpu.SemaphoreType.DMA((len(operands),)), pltpu.SemaphoreType.DMA((count,)), pltpu.SemaphoreType.DMA((count,))],
        compiler_params=pltpu.CompilerParams(collective_id=collective_id, has_side_effects=True),
        name="gather_weights",
    )(*operands)


def add_region(acc, temp, at, extra=()):
    ys, los, rows, columns = at
    chunk = 32
    per = rows.size // chunk

    def one(step, carry):
        del carry
        row = step % per * chunk
        lo = step // per % los.size
        y = step // (per * los.size)

        def view(ref, where):
            r = pl.ds(pl.multiple_of(where[2].start + row, 16), chunk)
            return ref.at[where[0].start + y, where[1].start + lo, r, where[3]]

        total = view(acc, at)[...].astype(jnp.float32)
        for t in extra:
            total += view(temp, t)[...].astype(jnp.float32)
        view(acc, at)[...] = total.astype(jnp.bfloat16)
        return 0

    lax.fori_loop(0, per * los.size * ys.size, one, 0)


def reduce_kernel(members, count, *refs):
    n = 1 + max(m[1] for m in members)
    grads, gain_in = refs[:n], refs[n]
    outs, gain_out = refs[n + 1:2 * n + 1], refs[2 * n + 1]
    accs, temps = refs[2 * n + 2:3 * n + 2], refs[3 * n + 2:4 * n + 2]
    gain_rings, local_sem, send, recv = refs[4 * n + 2:]
    place = torus_place()
    copies = Copies(send, recv)
    loads = []
    for i in range(n):
        load = pltpu.make_async_copy(grads[i], accs[i], local_sem.at[i])
        load.start()
        loads.append(load)
    barrier = pltpu.get_barrier_semaphore()
    far = device_at(shifted(place, "x", 2))
    sibling = device_at({**place, "core": 1 - place["core"]})
    others = [device_at(shifted(place, axis, by)) for axis in "xyz" for by in (1, -1)] + [far, sibling]
    for other in others:
        pl.semaphore_signal(barrier, inc=1, device_id=other, device_id_type=MESH)
    pl.semaphore_wait(barrier, len(others))
    parts = [[m for m in members if m[0] == part] for part in range(3)]

    def blocks(member, phase, at, half, landing):
        part, array, first, columns = member
        order = GATHER_ORDER[part]
        rows = accs[array].shape[2] // 2
        here = place
        if landing:
            for axis in order[phase + 1:]:
                here = shifted(here, axis, 1 if half else -1)
        return regions(here, order[phase], at % 4, order[:phase], columns, (half * rows, rows), first)

    def send_block(phase, part, at, half, by, land_at, slots):
        slots = iter(slots)
        device = device_at(shifted(place, GATHER_ORDER[part][phase], by))
        for m in parts[part]:
            for src, dst in zip(blocks(m, phase, at, half, False), blocks(m, phase, land_at, half, True)):
                copies.start(next(slots), accs[m[1]].at[src], temps[m[1]].at[dst], device)

    def wait_block(phase, part, half, by, land_at, slots):
        slots = iter(slots)
        device = device_at(shifted(place, GATHER_ORDER[part][phase], -by))
        for m in parts[part]:
            for dst in blocks(m, phase, land_at, half, True):
                copies.make(next(slots), temps[m[1]].at[dst], temps[m[1]].at[dst], device).wait_recv()

    def add_block(phase, part, at, half, land_ats):
        for m in parts[part]:
            where = blocks(m, phase, at, half, False)
            landed = [blocks(m, phase, land_at, half, True) for land_at in land_ats]
            for k, region in enumerate(where):
                add_region(accs[m[1]], temps[m[1]], region, [t[k] for t in landed])

    load = pltpu.make_async_copy(gain_in, gain_rings.at[0, place["core"]], local_sem.at[n])
    load.start()
    load.wait()
    slot = copies.slot(1)[0]
    copies.start(slot, gain_rings.at[0, place["core"]], gain_rings.at[0, place["core"]], sibling)
    copies.make(slot, gain_rings.at[0, 1 - place["core"]], gain_rings.at[0, 1 - place["core"]], sibling).wait_recv()
    gain_total = gain_rings[0, 0] + gain_rings[0, 1]

    for phase in (2, 1, 0):
        slots = {}
        for part in range(3):
            c = place[GATHER_ORDER[part][phase]]
            pieces = sum(len(blocks(m, phase, c, 0, False)) for m in parts[part])
            if phase == 2:
                for m in parts[part]:
                    if loads[m[1]] is not None:
                        loads[m[1]].wait()
                        loads[m[1]] = None
            for by in (1, -1):
                half = 0 if by == 1 else 1
                slots[part, by] = [copies.slot(pieces) for _ in range(3)]
                send_block(phase, part, c + 2, half, by, c + 2, slots[part, by][0])
            for by in (1, -1):
                half = 0 if by == 1 else 1
                send_block(phase, part, c + by, 1 - half, by, c + by if by == 1 else c + 1, slots[part, by][1])
        axis, ring = "zyx"[2 - phase], gain_rings.at[3 - phase]
        at = place[axis]
        ring[at] = gain_total
        gain_slots = copies.slot(3)
        for k, by in enumerate((1, -1)):
            copies.start(gain_slots[k], ring.at[at], ring.at[at], device_at(shifted(place, axis, by)))
        for part in range(3):
            c = place[GATHER_ORDER[part][phase]]
            for by in (1, -1):
                half = 0 if by == 1 else 1
                wait_block(phase, part, half, by, c + by, slots[part, by][0])
                add_block(phase, part, c + by, half, [c + by])
                send_block(phase, part, c + by, half, by, c + by if by == 1 else c + 1, slots[part, by][2])
        for k, by in enumerate((1, -1)):
            view = ring.at[(at - by) % 4]
            copies.make(gain_slots[k], view, view, device_at(shifted(place, axis, -by))).wait_recv()
        copies.start(gain_slots[2], ring.at[(at - 1) % 4], ring.at[(at - 1) % 4], device_at(shifted(place, axis, 1)))
        for part in range(3):
            c = place[GATHER_ORDER[part][phase]]
            for half in (0, 1):
                for by in (1, -1):
                    first = half == (0 if by == 1 else 1)
                    wait_block(phase, part, half, by, c if by == 1 else c + 2, slots[part, by][2 if first else 1])
                add_block(phase, part, c, half, [c, c + 2])
        view = ring.at[(at + 2) % 4]
        copies.make(gain_slots[2], view, view, device_at(shifted(place, axis, -1))).wait_recv()
        gain_total = (ring[0] + ring[1]) + (ring[2] + ring[3])
    gain_out[...] = gain_total
    finish_kernel(members, accs, outs, place, copies, local_sem)
    assert copies.used <= count, copies.used


def finish_kernel(members, accs, outs, place, copies, local_sem):
    n = len(members)

    def columns(i, x, z):
        _, _, first, width = members[i]
        step = width // 8
        return pl.ds(pl.multiple_of(first + ((x % 4) // 2 * 4 + z % 4) * step, 128), step)

    def block(i, x, z):
        return outs[members[i][1]].at[:, columns(i, x, z)]

    def halves(i, x, z, half):
        rows = outs[members[i][1]].shape[0] // 2
        return outs[members[i][1]].at[pl.ds(half * rows, rows), columns(i, x, z)]

    x, z = place["x"], place["z"]
    stores = []
    for i in range(n):
        store = pltpu.make_async_copy(accs[members[i][1]].at[place["y"], x % 2, :, columns(i, x, z)], block(i, x, z), local_sem.at[i])
        store.start()
        stores.append(store)
    for store in stores:
        store.wait()
    far = device_at(shifted(place, "x", 2))
    up, down = device_at(shifted(place, "z", 1)), device_at(shifted(place, "z", -1))
    slots = {name: copies.slot(n) for name in ("far", "up", "down", "far_up", "far_down", "two_up", "two_down", "far_two_up", "far_two_down")}

    def send(name, view, device):
        for i in range(n):
            copies.start(slots[name][i], view(i), view(i), device)

    def wait(name, view, device):
        for i in range(n):
            copies.make(slots[name][i], view(i), view(i), device).wait_recv()

    send("far", lambda i: block(i, x, z), far)
    send("up", lambda i: block(i, x, z), up)
    send("down", lambda i: block(i, x, z), down)
    wait("far", lambda i: block(i, x + 2, z), far)
    send("far_up", lambda i: block(i, x + 2, z), up)
    send("far_down", lambda i: block(i, x + 2, z), down)
    wait("up", lambda i: block(i, x, z - 1), down)
    send("two_up", lambda i: halves(i, x, z - 1, 0), up)
    wait("down", lambda i: block(i, x, z + 1), up)
    send("two_down", lambda i: halves(i, x, z + 1, 1), down)
    wait("far_up", lambda i: block(i, x + 2, z - 1), down)
    send("far_two_up", lambda i: halves(i, x + 2, z - 1, 0), up)
    wait("far_down", lambda i: block(i, x + 2, z + 1), up)
    send("far_two_down", lambda i: halves(i, x + 2, z + 1, 1), down)
    wait("two_up", lambda i: halves(i, x, z + 2, 0), down)
    wait("two_down", lambda i: halves(i, x, z + 2, 1), up)
    wait("far_two_up", lambda i: halves(i, x + 2, z + 2, 0), down)
    wait("far_two_down", lambda i: halves(i, x + 2, z + 2, 1), up)
    copies.finish()


def reduce_grads(grads, gain_grads, members, collective_id, count):
    shapes = [g.shape for g in grads]
    return pl.pallas_call(
        functools.partial(reduce_kernel, members, count),
        out_shape=[jax.ShapeDtypeStruct(s[2:], jnp.bfloat16) for s in shapes] + [jax.ShapeDtypeStruct(gain_grads.shape, jnp.float32)],
        in_specs=[pl.BlockSpec(memory_space=pl.ANY)] * (len(grads) + 1),
        out_specs=[pl.BlockSpec(memory_space=pl.ANY)] * len(grads) + [pl.BlockSpec(memory_space=pltpu.VMEM)],
        scratch_shapes=[pltpu.VMEM(s, jnp.bfloat16) for s in shapes] * 2
        + [pltpu.VMEM((4, 4) + gain_grads.shape, jnp.float32), pltpu.SemaphoreType.DMA((8,)),
           pltpu.SemaphoreType.DMA((count,)), pltpu.SemaphoreType.DMA((count,))],
        compiler_params=pltpu.CompilerParams(collective_id=collective_id, has_side_effects=True, vmem_limit_bytes=50 << 20),
        name="reduce_grads",
    )(*grads, gain_grads)


HEAD = 128
SPAN = 64
TILE = 256
score_scale = HEAD ** (-0.5)


def dot(a, b, a_dim, b_dim):
    return lax.dot_general(a, b, (((a_dim,), (b_dim,)), ((), ())), preferred_element_type=jnp.float32)


def gather_sorted(order_ref, seq, ref, column, width, out, out_at):
    for j in range(16):
        slot = order_ref[seq, j]
        rows = ref[slot // 2, 0, pl.ds(slot % 2 * SPAN, SPAN), column:column + width]
        out[out_at + j * SPAN:out_at + (j + 1) * SPAN, :] = rows


def tile_scores(q, k, low, high):
    scores = dot(q, k, 1, 1) * score_scale
    rows = lax.broadcasted_iota(jnp.int32, scores.shape, 0) % TILE + low
    keys = lax.broadcasted_iota(jnp.int32, scores.shape, 1)
    return jnp.where(keys <= rows, scores, -1e30)


def forward_kernel(order_ref, qkv_ref, out_ref, lse_ref, q_s, k_s, v_s):
    seq = pl.program_id(0)
    gather_sorted(order_ref, seq, qkv_ref, 0, HEAD, q_s.at[0], 0)
    gather_sorted(order_ref, seq, qkv_ref, HEAD, HEAD, q_s.at[1], 0)
    gather_sorted(order_ref, seq, qkv_ref, 2 * HEAD, HEAD, k_s, 0)
    gather_sorted(order_ref, seq, qkv_ref, 3 * HEAD, HEAD, v_s, 0)
    for i in range(1024 // TILE):
        low, high = i * TILE, (i + 1) * TILE
        q = q_s[:, low:high, :].reshape(2 * TILE, HEAD)
        scores = tile_scores(q, k_s[:high], low, high)
        top = jnp.max(scores, -1, keepdims=True)
        raised = jnp.exp(scores - top)
        total = jnp.sum(raised, -1, keepdims=True)
        probs = (raised * (1.0 / total)).astype(jnp.bfloat16)
        out = dot(probs, v_s[:high], 1, 0).astype(jnp.bfloat16)
        lse_ref[0, :, low:high, :] = jnp.broadcast_to(top + jnp.log(total), (2 * TILE, HEAD)).reshape(2, TILE, HEAD)
        for j in range(TILE // SPAN):
            slot = order_ref[seq, low // SPAN + j]
            for h in range(2):
                out_ref[slot // 2, 0, pl.ds(slot % 2 * SPAN, SPAN), h * HEAD:(h + 1) * HEAD] = out[
                    h * TILE + j * SPAN:h * TILE + (j + 1) * SPAN]


def attention_forward(order, qkv):
    return pl.pallas_call(
        forward_kernel,
        grid_spec=pltpu.PrefetchScalarGridSpec(
            num_scalar_prefetch=1, grid=(2,),
            in_specs=[pl.BlockSpec((8, 1, 128, 4 * HEAD), lambda s, order: (0, s, 0, 0))],
            out_specs=[pl.BlockSpec((8, 1, 128, 2 * HEAD), lambda s, order: (0, s, 0, 0)),
                       pl.BlockSpec((1, 2, 1024, HEAD), lambda s, order: (s, 0, 0, 0))],
            scratch_shapes=[pltpu.VMEM((2, 1024, HEAD), jnp.bfloat16), pltpu.VMEM((1024, HEAD), jnp.bfloat16), pltpu.VMEM((1024, HEAD), jnp.bfloat16)]),
        out_shape=[jax.ShapeDtypeStruct((8, 2, 128, 2 * HEAD), jnp.bfloat16), jax.ShapeDtypeStruct((2, 2, 1024, HEAD), jnp.float32)],
        compiler_params=pltpu.CompilerParams(vmem_limit_bytes=40 << 20),
        cost_estimate=pl.CostEstimate(flops=1400000000, bytes_accessed=6 << 20, transcendentals=3 << 20),
        name="attention_forward",
    )(order, qkv)


def backward_kernel(order_ref, qkv_ref, grad_ref, lse_ref, out_ref, q_s, k_s, v_s, g_s, dk_s, dv_s):
    seq = pl.program_id(0)
    gather_sorted(order_ref, seq, qkv_ref, 0, HEAD, q_s.at[0], 0)
    gather_sorted(order_ref, seq, qkv_ref, HEAD, HEAD, q_s.at[1], 0)
    gather_sorted(order_ref, seq, qkv_ref, 2 * HEAD, HEAD, k_s, 0)
    gather_sorted(order_ref, seq, qkv_ref, 3 * HEAD, HEAD, v_s, 0)
    gather_sorted(order_ref, seq, grad_ref, 0, HEAD, g_s.at[0], 0)
    gather_sorted(order_ref, seq, grad_ref, HEAD, HEAD, g_s.at[1], 0)
    tiles = 1024 // TILE
    for i in reversed(range(tiles)):
        low, high = i * TILE, (i + 1) * TILE
        q = q_s[:, low:high, :].reshape(2 * TILE, HEAD)
        g = g_s[:, low:high, :].reshape(2 * TILE, HEAD)
        k, v = k_s[:high], v_s[:high]
        lse = lse_ref[0, :, low:high, :].reshape(2 * TILE, HEAD)[:, :1]
        probs = jnp.exp(tile_scores(q, k, low, high) - lse)
        grad_probs = dot(g, v, 1, 1)
        inner = jnp.sum(probs * grad_probs, -1, keepdims=True)
        grad_scores = (probs * (grad_probs - inner)).astype(jnp.bfloat16)
        probs_low = probs.astype(jnp.bfloat16)
        dq = (dot(grad_scores, k, 1, 0) * score_scale).astype(jnp.bfloat16)
        dk = dot(grad_scores, q, 0, 0)
        dv = dot(probs_low, g, 0, 0)
        if i == tiles - 1:
            dk_s[...] = dk
            dv_s[...] = dv
        else:
            dk_s[:high] += dk
            dv_s[:high] += dv
        for j in range(TILE // SPAN):
            slot = order_ref[seq, low // SPAN + j]
            for h in range(2):
                out_ref[slot // 2, 0, pl.ds(slot % 2 * SPAN, SPAN), h * HEAD:(h + 1) * HEAD] = dq[
                    h * TILE + j * SPAN:h * TILE + (j + 1) * SPAN]
    for j in range(16):
        slot = order_ref[seq, j]
        rows = pl.ds(slot % 2 * SPAN, SPAN)
        at = slice(j * SPAN, (j + 1) * SPAN)
        out_ref[slot // 2, 0, rows, 2 * HEAD:3 * HEAD] = (dk_s[at] * score_scale).astype(jnp.bfloat16)
        out_ref[slot // 2, 0, rows, 3 * HEAD:] = dv_s[at].astype(jnp.bfloat16)


def attention_backward(order, qkv, grad, lse):
    return pl.pallas_call(
        backward_kernel,
        grid_spec=pltpu.PrefetchScalarGridSpec(
            num_scalar_prefetch=1, grid=(2,),
            in_specs=[pl.BlockSpec((8, 1, 128, 4 * HEAD), lambda s, order: (0, s, 0, 0)),
                      pl.BlockSpec((8, 1, 128, 2 * HEAD), lambda s, order: (0, s, 0, 0)),
                      pl.BlockSpec((1, 2, 1024, HEAD), lambda s, order: (s, 0, 0, 0))],
            out_specs=pl.BlockSpec((8, 1, 128, 4 * HEAD), lambda s, order: (0, s, 0, 0)),
            scratch_shapes=[pltpu.VMEM((2, 1024, HEAD), jnp.bfloat16), pltpu.VMEM((1024, HEAD), jnp.bfloat16), pltpu.VMEM((1024, HEAD), jnp.bfloat16),
                            pltpu.VMEM((2, 1024, HEAD), jnp.bfloat16), pltpu.VMEM((1024, HEAD), jnp.float32), pltpu.VMEM((1024, HEAD), jnp.float32)]),
        out_shape=jax.ShapeDtypeStruct((8, 2, 128, 4 * HEAD), jnp.bfloat16),
        compiler_params=pltpu.CompilerParams(vmem_limit_bytes=40 << 20),
        cost_estimate=pl.CostEstimate(flops=3400000000, bytes_accessed=8 << 20, transcendentals=3 << 20),
        name="attention_backward",
    )(order, qkv, grad, lse)


HEADS = 16
KV_HEADS = 8
rope_base = 1000000.0
norm_eps = 1e-06
ROWS = 256
WIDTH = 1024
QUERY = HEADS * HEAD
KEY = KV_HEADS * HEAD
FF = 3072


def load_pair(own, sibling, buffer, core, sems):
    copies = [pltpu.make_async_copy(own, buffer.at[:, core], sems.at[0]),
              pltpu.make_async_copy(sibling, buffer.at[:, 1 - core], sems.at[1])]
    for copy in copies:
        copy.start()
    return copies


def wait_all_of(copies):
    for copy in copies:
        copy.wait()


def inverse_rms(values):
    return lax.rsqrt(jnp.mean(values * values, -1, keepdims=True) + norm_eps)


def rms_back(values, inverse, norm_gain, upstream):
    scaled = upstream * norm_gain
    inner = jnp.mean(scaled * values, -1, keepdims=True)
    grad_gain = jnp.sum(upstream * values * inverse, 0, keepdims=True)
    return inverse * scaled - values * (inverse * inverse * inverse * inner), grad_gain


def store_stripes(rows, scratch, width):
    turned = rows.T
    stripe = width // 16
    for j in range(16):
        scratch[j // 2, j % 2] = turned[j * stripe:(j + 1) * stripe]


def project_kernel(core_ref, x_ref, own_ref, sib_ref, qg_ref, kg_ref, cos_ref, sin_ref,
                   sent_ref, q_raw_ref, k_raw_ref, x_own_ref, x_sib_ref, w_s, x_s, sems):
    core = core_ref[0]
    loads = load_pair(own_ref, sib_ref, w_s, core, sems)
    x = x_ref[...]
    store_stripes(x, x_s, WIDTH)
    x_own_ref[...] = x_s[:, core]
    x_sib_ref[...] = x_s[:, 1 - core]
    wait_all_of(loads)

    def block(n, carry):
        at = pl.ds(pl.multiple_of(n * 512, 512), 512)
        q_raw_ref[:, at] = dot(x, w_s[:, :, :, at].reshape(WIDTH, 512), 1, 0)
        return carry

    lax.fori_loop(0, 4, block, 0)
    for n in range(2):
        at = slice(n * 512, (n + 1) * 512)
        k_raw_ref[:, at] = dot(x, w_s[:, :, :, QUERY + n * 512:QUERY + (n + 1) * 512].reshape(WIDTH, 512), 1, 0)
    for n in range(2):
        value = dot(x, w_s[:, :, :, QUERY + KEY + n * 512:QUERY + KEY + (n + 1) * 512].reshape(WIDTH, 512), 1, 0).astype(jnp.bfloat16)
        for h in range(4):
            sent_ref[4 * n + h, :, :, 3 * HEAD:] = value[:, h * HEAD:(h + 1) * HEAD].reshape(2, 128, HEAD)
    cosine, sine = cos_ref[...], sin_ref[...]

    def place_heads(raw_ref, gain_ref, heads, column, each):
        inverse = inverse_rms(raw_ref[...])
        for h in range(heads):
            at = slice(h * HEAD, (h + 1) * HEAD)
            normed = raw_ref[:, at] * inverse * gain_ref[:, at]
            turned = normed * cosine + pltpu.roll(normed, HEAD // 2, 1) * sine
            first = column + h % each * HEAD
            sent_ref[h // each, :, :, first:first + HEAD] = turned.astype(jnp.bfloat16).reshape(2, 128, HEAD)

    place_heads(q_raw_ref, qg_ref, HEADS, 0, 2)
    place_heads(k_raw_ref, kg_ref, KV_HEADS, 2 * HEAD, 1)


def vmem(n):
    return [pl.BlockSpec(memory_space=pltpu.VMEM)] * n


def anywhere(n):
    return [pl.BlockSpec(memory_space=pl.ANY)] * n


SMEM = pl.BlockSpec(memory_space=pltpu.SMEM)
BF16 = jnp.bfloat16
F32 = jnp.float32


def project(core, rows, own, sibling, q_gain, k_gain, cosine, sine):
    return pl.pallas_call(
        project_kernel,
        in_specs=[SMEM] + vmem(1) + anywhere(2) + vmem(4),
        out_specs=vmem(5),
        out_shape=[jax.ShapeDtypeStruct((8, 2, 128, 4 * HEAD), BF16), jax.ShapeDtypeStruct((ROWS, QUERY), F32),
                   jax.ShapeDtypeStruct((ROWS, KEY), F32), jax.ShapeDtypeStruct((8, 64, ROWS), BF16), jax.ShapeDtypeStruct((8, 64, ROWS), BF16)],
        scratch_shapes=[pltpu.VMEM((8, 2, 64, 4096), BF16), pltpu.VMEM((8, 2, 64, ROWS), BF16), pltpu.SemaphoreType.DMA((2,))],
        compiler_params=pltpu.CompilerParams(vmem_limit_bytes=40 << 20),
        cost_estimate=pl.CostEstimate(flops=2200000000, bytes_accessed=16 << 20, transcendentals=0),
        name="project",
    )(core, rows, own, sibling, q_gain, k_gain, cosine, sine)


def middle_kernel(core_ref, heads_ref, x_ref, cot_ref, ag_ref, fg_ref, wo_own, wo_sib, wgu_own, wgu_sib, wd_own, wd_sib,
                  layer_ref, grad_heads_ref, grad_mixed_ref, grad_branch_ref, grad_gu_ref, grad_ffn_ref, gains_ref,
                  att_own_ref, att_sib_ref, mix_own_ref, mix_sib_ref, mid_own_ref, mid_sib_ref,
                  wo_s, wgu_s, wd_s, att_s, gu_s, branch_s, mixed_s, low_s, mid_s, ffn_s, att_t, mix_t, mid_t, sems):
    core = core_ref[0]
    load_o = load_pair(wo_own, wo_sib, wo_s, core, sems.at[0])
    load_gu = load_pair(wgu_own, wgu_sib, wgu_s, core, sems.at[1])
    load_d = load_pair(wd_own, wd_sib, wd_s, core, sems.at[2])
    for g in range(8):
        att_s[:, g * 256:(g + 1) * 256] = heads_ref[g].reshape(ROWS, 256)
    store_stripes(att_s[...], att_t, QUERY)
    wait_all_of(load_o)
    for n in range(2):
        at = slice(n * 512, (n + 1) * 512)
        branch_s[:, at] = dot(att_s[...], wo_s[:, :, :, at].reshape(QUERY, 512), 1, 0)
    branch_inverse = inverse_rms(branch_s[...])
    mixed = x_ref[...].astype(F32) + branch_s[...] * branch_inverse * ag_ref[...]
    mixed_s[...] = mixed
    low_s[...] = mixed.astype(BF16)
    store_stripes(low_s[...], mix_t, WIDTH)
    wait_all_of(load_gu)

    def forward_block(n, carry):
        at = pl.ds(pl.multiple_of(n * 512, 512), 512)
        up_at = pl.ds(pl.multiple_of(FF + n * 512, 512), 512)
        gate = dot(low_s[...], wgu_s[:, :, :, at].reshape(WIDTH, 512), 1, 0)
        up = dot(low_s[...], wgu_s[:, :, :, up_at].reshape(WIDTH, 512), 1, 0)
        gu_s[:, at] = gate
        gu_s[:, up_at] = up
        mid_s[:, at] = (gate * jax.nn.sigmoid(gate) * up).astype(BF16)
        return carry

    lax.fori_loop(0, FF // 512, forward_block, 0)
    wait_all_of(load_d)
    for n in range(2):
        at = slice(n * 512, (n + 1) * 512)
        ffn_s[:, at] = dot(mid_s[...], wd_s[:, :, :, at].reshape(FF, 512), 1, 0)
    store_stripes(mid_s[...], mid_t, FF)
    ffn_out = ffn_s[...]
    ffn_inverse = inverse_rms(ffn_out)
    layer_ref[...] = (mixed_s[...] + ffn_out * ffn_inverse * fg_ref[...]).astype(BF16)
    grad_ffn, grad_ffn_gain = rms_back(ffn_out, ffn_inverse, fg_ref[...], cot_ref[...].astype(F32))
    grad_ffn_ref[...] = grad_ffn.astype(BF16)

    def backward_block(n, carry):
        at = pl.ds(pl.multiple_of(n * 768, 256), 768)
        up_at = pl.ds(pl.multiple_of(FF + n * 768, 256), 768)
        grad_middle = dot(grad_ffn_ref[...], wd_s[pl.ds(n * 2, 2)].reshape(768, WIDTH), 1, 1)
        gate, up = gu_s[:, at], gu_s[:, up_at]
        sigmoid_gate = jax.nn.sigmoid(gate)
        grad_gu_ref[:, at] = (grad_middle * up * sigmoid_gate * (1.0 + gate * (1.0 - sigmoid_gate))).astype(BF16)
        grad_gu_ref[:, up_at] = (grad_middle * (gate * sigmoid_gate)).astype(BF16)
        return carry

    lax.fori_loop(0, 4, backward_block, 0)
    for n in range(4):
        at = slice(n * 256, (n + 1) * 256)
        ffn_s[:, at] = cot_ref[:, at].astype(F32) + dot(grad_gu_ref[...], wgu_s[2 * n:2 * n + 2].reshape(256, 2 * FF), 1, 1)
    grad_mixed_ref[...] = ffn_s[...]
    grad_branch, grad_attn_gain = rms_back(branch_s[...], branch_inverse, ag_ref[...], ffn_s[...])
    grad_branch_ref[...] = grad_branch.astype(BF16)
    for g in range(8):
        grad = dot(grad_branch_ref[...], wo_s[g].reshape(256, WIDTH), 1, 1)
        grad_heads_ref[g] = grad.astype(BF16).reshape(2, 128, 256)
    gains_ref[...] = jnp.zeros_like(gains_ref)
    gains_ref[0:1] = grad_attn_gain
    gains_ref[1:2] = grad_ffn_gain
    for own, sib, turned in ((att_own_ref, att_sib_ref, att_t), (mix_own_ref, mix_sib_ref, mix_t), (mid_own_ref, mid_sib_ref, mid_t)):
        own[...] = turned[:, core]
        sib[...] = turned[:, 1 - core]


def middle(core, heads, rows, cotangent, a_gain, f_gain, wo, wgu, wd):
    def stripes(width):
        return [jax.ShapeDtypeStruct((8, width // 16, ROWS), BF16)] * 2

    return pl.pallas_call(
        middle_kernel,
        in_specs=[SMEM] + vmem(5) + anywhere(6),
        out_specs=vmem(13),
        out_shape=[jax.ShapeDtypeStruct((ROWS, WIDTH), BF16), jax.ShapeDtypeStruct((8, 2, 128, 256), BF16), jax.ShapeDtypeStruct((ROWS, WIDTH), F32),
                   jax.ShapeDtypeStruct((ROWS, WIDTH), BF16), jax.ShapeDtypeStruct((ROWS, 2 * FF), BF16), jax.ShapeDtypeStruct((ROWS, WIDTH), BF16),
                   jax.ShapeDtypeStruct((8, WIDTH), F32)] + stripes(QUERY) + stripes(WIDTH) + stripes(FF),
        scratch_shapes=[pltpu.VMEM((8, 2, 128, WIDTH), BF16), pltpu.VMEM((8, 2, 64, 2 * FF), BF16), pltpu.VMEM((8, 2, 192, WIDTH), BF16),
                        pltpu.VMEM((ROWS, QUERY), BF16), pltpu.VMEM((ROWS, 2 * FF), F32), pltpu.VMEM((ROWS, WIDTH), F32), pltpu.VMEM((ROWS, WIDTH), F32),
                        pltpu.VMEM((ROWS, WIDTH), BF16), pltpu.VMEM((ROWS, FF), BF16), pltpu.VMEM((ROWS, WIDTH), F32),
                        pltpu.VMEM((8, 2, 128, ROWS), BF16), pltpu.VMEM((8, 2, 64, ROWS), BF16), pltpu.VMEM((8, 2, 192, ROWS), BF16),
                        pltpu.SemaphoreType.DMA((3, 2))],
        compiler_params=pltpu.CompilerParams(vmem_limit_bytes=60 << 20),
        cost_estimate=pl.CostEstimate(flops=12000000000, bytes_accessed=40 << 20, transcendentals=3 << 20),
        name="middle",
    )(core, heads, rows, cotangent, a_gain, f_gain, *wo, *wgu, *wd)


def last_kernel(core_ref, grad_ref, q_raw_ref, k_raw_ref, mixed_ref, qg_ref, kg_ref, cos_ref, sin_ref, own_ref, sib_ref,
                tokens_ref, grad_out_ref, gains_ref, w_s, dy_s, sems):
    loads = load_pair(own_ref, sib_ref, w_s, core_ref[0], sems)
    cosine, sine = cos_ref[...], sin_ref[...]

    def one(raw_ref, gain_ref, heads, column, each, out_at):
        width = heads * HEAD
        for h in range(heads):
            first = column + h % each * HEAD
            u = grad_ref[h // each, :, :, first:first + HEAD].reshape(ROWS, HEAD).astype(F32)
            dy_s[:, h * HEAD:(h + 1) * HEAD] = u * cosine - pltpu.roll(u, HEAD // 2, 1) * sine
        raw = raw_ref[...]
        grad, grad_gain = rms_back(raw, inverse_rms(raw), gain_ref[...], dy_s[:, :width])
        grad_out_ref[:, out_at:out_at + width] = grad.astype(BF16)
        return grad_gain

    q_gain = one(q_raw_ref, qg_ref, HEADS, 0, 2, 0)
    k_gain = one(k_raw_ref, kg_ref, KV_HEADS, 2 * HEAD, 1, QUERY)
    for g in range(8):
        grad_out_ref[:, QUERY + KEY + g * HEAD:QUERY + KEY + (g + 1) * HEAD] = grad_ref[g, :, :, 3 * HEAD:].reshape(ROWS, HEAD)
    gains_ref[...] = jnp.zeros_like(gains_ref)
    gains_ref[0:1] = q_gain[:, :WIDTH]
    gains_ref[1:2] = q_gain[:, WIDTH:]
    gains_ref[2:3] = k_gain
    wait_all_of(loads)
    for n in range(4):
        at = slice(n * 256, (n + 1) * 256)
        tokens_ref[:, at] = (mixed_ref[:, at] + dot(grad_out_ref[...], w_s[2 * n:2 * n + 2].reshape(256, 4096), 1, 1)).astype(BF16)


def last(core, grad, q_raw, k_raw, grad_mixed, q_gain, k_gain, cosine, sine, own, sibling):
    return pl.pallas_call(
        last_kernel,
        in_specs=[SMEM] + vmem(8) + anywhere(2),
        out_specs=vmem(3),
        out_shape=[jax.ShapeDtypeStruct((ROWS, WIDTH), BF16), jax.ShapeDtypeStruct((ROWS, 4096), BF16), jax.ShapeDtypeStruct((8, WIDTH), F32)],
        scratch_shapes=[pltpu.VMEM((8, 2, 64, 4096), BF16), pltpu.VMEM((ROWS, QUERY), F32), pltpu.SemaphoreType.DMA((2,))],
        compiler_params=pltpu.CompilerParams(vmem_limit_bytes=40 << 20),
        cost_estimate=pl.CostEstimate(flops=2200000000, bytes_accessed=16 << 20, transcendentals=0),
        name="last",
    )(core, grad, q_raw, k_raw, grad_mixed, q_gain, k_gain, cosine, sine, own, sibling)
MEMBERS = ((1, 0, 0, 2048), (2, 0, 2048, 1024), (2, 0, 3072, 1024), (0, 1, 0, 1024), (0, 2, 0, 3072), (1, 2, 3072, 3072), (2, 3, 0, 1024))


def angles(positions):
    steps_half = jnp.arange(HEAD // 2, dtype=jnp.float32)
    inverse_freq = rope_base ** (-2.0 * steps_half / HEAD)
    phase = positions.astype(jnp.float32)[..., None] * inverse_freq
    cosine, sine = jnp.cos(phase), jnp.sin(phase)
    return jnp.concatenate([cosine, cosine], -1), jnp.concatenate([-sine, sine], -1)


def to_sibling(array):
    return lax.ppermute(array, "fsdp", [(i, i ^ 1) for i in range(16)])


def weight_grad(own, sibling, grad_rows):
    count = own.shape[1]
    from_sibling = to_sibling(dot(sibling.reshape(8 * count, ROWS), grad_rows, 1, 0).astype(BF16))
    total = (dot(own.reshape(8 * count, ROWS), grad_rows, 1, 0) + from_sibling.astype(F32)).astype(BF16)
    return total.reshape(4, 2, count, total.shape[1])


def per_device(
    tokens,
    span_order,
    w_query,
    w_key,
    w_value,
    w_out,
    w_gate,
    w_up,
    w_down,
    query_gain,
    key_gain,
    attn_gain,
    ffn_gain,
    cotangent,
):
    seq_local, rows_local, width = tokens.shape
    span_rows = rows_local // 2
    at_fsdp = lax.axis_index("fsdp")
    core = (at_fsdp % 2).astype(jnp.int32).reshape(1)
    token_rows = tokens.reshape(ROWS, width)

    gains_here = jnp.concatenate([query_gain, key_gain, attn_gain, ffn_gain, jnp.zeros((704,), F32)])
    *gathered, gains_all = gather_weights(
        (w_query, w_key, w_value, w_out, w_gate, w_up, w_down), tuple(m[:3] for m in MEMBERS), gains_here.reshape(8, 128), 1, 200)
    own_weights = [w.reshape((8,) + w.shape[2:]) for w in gathered]
    wqkv, wo, wgu, wd = [(w, to_sibling(w)) for w in own_weights]
    gains_all = gains_all.reshape(16, 1024)
    q_gain_all = gains_all[:, :128].reshape(1, QUERY)
    k_gain_all = gains_all[:, 128:192].reshape(1, KEY)
    a_gain_all = gains_all[:, 192:256].reshape(1, WIDTH)
    f_gain_all = gains_all[:, 256:320].reshape(1, WIDTH)

    own_spans = lax.dynamic_slice_in_dim(span_order, 2 * lax.axis_index("ctx"), 2, 1)
    offsets = jnp.arange(span_rows, dtype=jnp.int32)
    cosine, sine = angles((own_spans[:, :, None] * span_rows + offsets).reshape(ROWS))
    numbers = jnp.arange(16, dtype=jnp.int32)
    slot_of = jnp.sum(jnp.where(span_order[:, :, None] == numbers, numbers[None, :, None], 0), 1)

    def exchange(array):
        return lax.all_to_all(array, "ctx", split_axis=0, concat_axis=0, tiled=True)

    sent, query_raw, key_raw, tok_own, tok_sib = project(core, token_rows, *wqkv, q_gain_all, k_gain_all, cosine, sine)
    qkv = exchange(sent)
    out_heads, lse = attention_forward(slot_of, qkv)
    (layer_out, grad_sent, grad_mixed, grad_branch, grad_gu, grad_ffn, gains_af,
     att_own, att_sib, mix_own, mix_sib, mid_own, mid_sib) = middle(
        core, exchange(out_heads), token_rows, cotangent.reshape(ROWS, width), a_gain_all, f_gain_all, wo, wgu, wd)
    grad_heads = exchange(grad_sent)
    shard_down = weight_grad(mid_own, mid_sib, grad_ffn)
    shard_gu = weight_grad(mix_own, mix_sib, grad_gu)
    shard_out = weight_grad(att_own, att_sib, grad_branch)
    grad_qkv_heads = attention_backward(slot_of, qkv, grad_heads, lse)
    grad_tokens, grad_qkv, gains_qk = last(
        core, exchange(grad_qkv_heads), query_raw, key_raw, grad_mixed, q_gain_all, k_gain_all, cosine, sine, *wqkv)
    shard_qkv = weight_grad(tok_own, tok_sib, grad_qkv)
    gain_grads = jnp.concatenate([gains_qk[:3], gains_af[:2], jnp.zeros((3, WIDTH), F32)])
    *totals, gain_totals = reduce_grads((shard_qkv, shard_out, shard_gu, shard_down), gain_grads, MEMBERS, 2, 400)
    qkv_total, out_total, gu_total, down_total = [t.astype(F32) for t in totals]
    gain_totals = gain_totals.reshape(-1)

    def own_gain(first, count):
        return lax.dynamic_slice_in_dim(gain_totals, first + at_fsdp * count, count)

    return (
        layer_out.reshape(tokens.shape),
        grad_tokens.reshape(tokens.shape),
        qkv_total[:, :QUERY],
        qkv_total[:, QUERY:QUERY + KEY],
        qkv_total[:, QUERY + KEY:],
        out_total,
        gu_total[:, :FF],
        gu_total[:, FF:],
        down_total,
        own_gain(0, 128),
        own_gain(2048, 64),
        own_gain(3072, 64),
        own_gain(4096, 64),
    )


def solution(mesh):
    rows, shard, gain = P("fsdp", "ctx", None), P("fsdp", None), P("fsdp")
    return jax.shard_map(
        per_device,
        mesh=mesh,
        in_specs=(rows, shard) + (shard,) * 7 + (gain,) * 4 + (rows,),
        out_specs=(rows, rows) + (shard,) * 7 + (gain,) * 4,
        check_vma=False,
    )
```

time: 613 us -> 430 us (0.70)
  local copies, waits for them, and re-layouts: 99.9 us -> 29.3 us
  blocking collectives: 65.4 us -> 0 us
  matrix products: 98.8 us -> 35.7 us
  other arithmetic: 52.9 us -> 3.47 us
  Pallas kernels: 203 us -> 247 us
  waiting for transfers between devices: 63.3 us -> 84.3 us
    psum x1 -> x0, blocking collectives: 65.4 us -> none  [per_device(): lax.psum(jnp.concatenate([grad_query_gain, grad_key_gain, grad_attn_gain,...]
    dot_general x42 -> x8, matrix products: 98.8 us -> 35.7 us  [dot(): lax.dot_general(a, b, (((a_dim,), (b_dim,)), ((), ())), preferred_element...]
    pallas_call x2 -> x5, Pallas kernels: 183 us -> 227 us  [the longest x1 103 us: reduce_grads(): pl.pallas_call(functools.partial(reduce_kernel, members, count), out_shap...]
    convert_element_type x16 -> x2, other arithmetic: 23.3 us -> 1.81 us  [per_device(): qkv_total, out_total, gu_total, down_total = [t.astype(F32) for t in totals]]
    convert_element_type x6 -> x1, local copies, waits for them, and re-layouts: 14.9 us -> 0.08 us  [angles(): phase = positions.astype(jnp.float32)[..., None] * inverse_freq]
    another operation x8 -> x0, local copies, waits for them, and re-layouts: 13 us -> none  [the longest x3 7.2 us: split_columns(): rows.reshape(count, 8, 2, stripe).transpose(2, 0, 1, 3)]
    select_n x6 -> x0, local copies, waits for them, and re-layouts: 11.3 us -> none  [the longest x3 6.05 us: join_columns(): even = jnp.where(core == 0, own, sibling)]
    ppermute x14 -> x8, waiting for transfers between devices: 0.04 us -> 11.1 us  [to_sibling(): return lax.ppermute(array, 'fsdp', [(i, i ^ 1) for i in range(16)])]
  transfers between devices with their start and end apart: 18 -> 12, of which waited for: 4 -> 6; matrix products, arithmetic and copies ran while one was open for 24% -> 8% of each run, Pallas kernels for 3% -> 8%
where the time goes in v2:
time: 430 us; the launch traced here: 422 us
  Pallas kernels  247 us (57%)
  waiting for transfers between devices  84.3 us (20%)
  matrix products  35.7 us (8%)
  local copies, waits for them, and re-layouts  29.3 us (7%)
  starting transfers between devices  20.6 us (5%)
    pallas_call x1, Pallas kernels, reduce_grads(): pl.pallas_call(functools.partial(reduce_kernel, members, count), out_shap...  103 us
    pallas_call x1, Pallas kernels, gather_weights(): pl.pallas_call(functools.partial(gather_kernel, members, gains, count), o...  85.4 us
    all_to_all x4, waiting for transfers between devices, exchange(): return lax.all_to_all(array, 'ctx', split_axis=0, concat_axis=0, tiled=True)  73.2 us
    dot_general x8, matrix products, dot(): lax.dot_general(a, b, (((a_dim,), (b_dim,)), ((), ())), preferred_element...  35.7 us
    pallas_call x1, Pallas kernels, middle(): pl.pallas_call(middle_kernel, in_specs=[SMEM] + vmem(5) + anywhere(6), ou...  25.9 us
    unnamed x50, local copies, waits for them, and re-layouts  21.3 us
    all_to_all x4, starting transfers between devices, exchange(): return lax.all_to_all(array, 'ctx', split_axis=0, concat_axis=0, tiled=True)  18.5 us
    pallas_call x1, Pallas kernels, attention_backward(): pl.pallas_call(backward_kernel, grid_spec=pltpu.PrefetchScalarGridSpec(nu...  11.8 us
  transfers between devices with their start and end apart: 12, of which 6 were waited for; matrix products, arithmetic and copies ran while one was open for 8% of the time, Pallas kernels for 8%

profile of v2, /device:TPU:0, one launch (start us, length us, event | category | flops | bytes accessed | tf_op | source)
XLA Modules:
  0.0 421.7 jit_solution(14545941919810770258)
XLA Ops:
  0.7 1.4 concatenate.12
  2.0 85.4 %gather_weights.1 = (bf16[4,2,64,4096]{3,2,1,0:T(8,128)(2,1)}, bf16[4,2,128,1024]{3,2,1,0:T(8,128)(2,1)}, bf16[4,2,64,6144]{3,2,1,0:T(8,128)(2,1)}, bf16[4,2,192...) custom-call(bf16[64,2048]{1,0:T(8,128)(2,1)} %refs_0_.1, bf16[64,1024]{1,0:T(8,128)(2,1)} %refs_1_.1, bf16[64,1024]{1,0:T(8,128)(2,1)} %refs_2_.1, ...), custom_call_target="tpu_custom_call" | custom-call | tf_op jit(solution)/shard_map/gather_weights/pallas_call | solution.py:186
  88.4 0.8 dynamic-slice_multiply_fusion
  89.3 0.9 copy.31
  91.0 4.0 collective-permute-done.sib_ref
  95.1 2.2 copy-done
  97.2 1.0 copy-done.12
  98.3 6.0 %project.1 = (bf16[8,2,128,512]{3,2,1,0:T(8,128)(2,1)S(1)}, f32[256,2048]{1,0:T(8,128)S(1)}, f32[256,1024]{1,0:T(8,128)S(1)}, bf16[8,64,256]{2,1,0:T(8,128)(2,1)S(1)}, bf16[8,64,256]{2,1,0:T(8,128)(2,1)S(1)}) custom-call(s32[1]{0:T(128)} %bitcast.core_ref, bf16[256,1024]{1,0:T(8,128)(2,1)S(1)} %bitcast.54, bf16[8,64,4096]{2,1,0:T(8,128)(2,1)S(1)} %bitcast.49, ...), custom_call_target="tpu_custom_call" | custom-call | flops 2200000000 | bytes 16777216 | tf_op jit(solution)/shard_map/project/pallas_call | solution.py:619
  104.3 1.3 copy-done.4
  105.6 1.3 copy-done.6
  107.0 0.7 copy-done.10
  108.4 5.0 %all-to-all-start = ((bf16[8,2,128,512]{3,2,1,0:T(8,128)(2,1)}), bf16[8,2,128,512]{3,2,1,0:T(8,128)(2,1)S(1)}, u32[]{:S(2)}, u32[]{:S(2)}) async-start(bf16[8,2,128,512]{3,2,1,0:T(8,128)(2,1)} %copy-done.6), calls=%async_computation | async-start | bytes 4194304 | tf_op jit(solution)/shard_map/all_to_all | solution.py:829
  113.6 26.8 %all-to-all-done.qkv_ref = bf16[8,2,128,512]{3,2,1,0:T(8,128)(2,1)S(1)} async-done(((bf16[8,2,128,512]{3,2,1,0:T(8,128)(2,1)}), bf16[8,2,128,512]{3,2,1,0:T(8,128)(2,1)S(1)}, u32[]{:S(2)}, u32[]{:S(2)}) %all-to-all-start) | async-done | bytes 2097184 | tf_op jit(solution)/shard_map/all_to_all | solution.py:829
  140.3 8.2 %attention_forward.1 = (bf16[8,2,128,256]{3,2,1,0:T(8,128)(2,1)S(1)}, f32[2,2,1024,128]{3,2,1,0:T(8,128)S(1)}) custom-call(s32[2,16]{1,0:T(2,128)S(1)} %select_reduce_fusion.order_ref, bf16[8,2,128,512]{3,2,1,0:T(8,128)(2,1)S(1)} %all-to-all-done.qkv_ref), custom_call_target="tpu_custom_call" | custom-call | flops 1400000000 | bytes 6291456 | tf_op jit(solution)/shard_map/attention_forward/pallas_call | solution.py:450
  148.5 1.0 copy-done.9
  149.5 1.3 copy-done.15
  150.9 5.0 %all-to-all-start.1 = ((bf16[8,2,128,256]{3,2,1,0:T(8,128)(2,1)}), bf16[8,2,128,256]{3,2,1,0:T(8,128)(2,1)}, u32[]{:S(2)}, u32[]{:S(2)}) async-start(bf16[8,2,128,256]{3,2,1,0:T(8,128)(2,1)} %copy-done.9), calls=%async_computation.1 | async-start | bytes 2097152 | tf_op jit(solution)/shard_map/all_to_all | solution.py:829
  157.2 14.6 %all-to-all-done.1.heads_ref = bf16[8,2,128,256]{3,2,1,0:T(8,128)(2,1)} async-done(((bf16[8,2,128,256]{3,2,1,0:T(8,128)(2,1)}), bf16[8,2,128,256]{3,2,1,0:T(8,128)(2,1)}, u32[]{:S(2)}, u32[]{:S(2)}) %all-to-all-start.1) | async-done | bytes 1048608 | tf_op jit(solution)/shard_map/all_to_all | solution.py:829
  171.8 25.9 %middle.1 = (bf16[256,1024]{1,0:T(8,128)(2,1)}, bf16[8,2,128,256]{3,2,1,0:T(8,128)(2,1)}, f32[256,1024]{1,0:T(8,128)}, bf16[256,1024]{1,0:T(8,128)(2,1)}, bf16[2...) custom-call(s32[1]{0:T(128)} %bitcast.core_ref, ...), custom_call_target="tpu_custom_call" | custom-call | flops 12000000000 | bytes 41943040 | tf_op jit(solution)/shard_map/middle/pallas_call | solution.py:708
  197.7 4.2 %all-to-all-start.2 = ((bf16[8,2,128,256]{3,2,1,0:T(8,128)(2,1)}), bf16[8,2,128,256]{3,2,1,0:T(8,128)(2,1)}, u32[]{:S(2)}, u32[]{:S(2)}) async-start(bf16[8,2,128,256]{3,2,1,0:T(8,128)(2,1)} %get-tuple-element.54), calls=%async_computation.2 | async-start | bytes 2097152 | tf_op jit(solution)/shard_map/all_to_all | solution.py:829
  201.9 6.5 %convolution_convert_fusion = bf16[512,6144]{1,0:T(8,128)(2,1)} fusion(bf16[512,256]{1,0:T(8,128)(2,1)} %bitcast.67, bf16[256,6144]{1,0:T(8,128)(2,1)} %get-tuple-element.67), kind=kOutput, calls=%fused_computation.1 | convolution fusion | flops 1613758464 | bytes 9699328 | tf_op jit(solution)/shard_map/dot_general | solution.py:409
  208.6 9.3 %all-to-all-done.2.grad_ref = bf16[8,2,128,256]{3,2,1,0:T(8,128)(2,1)} async-done(((bf16[8,2,128,256]{3,2,1,0:T(8,128)(2,1)}), bf16[8,2,128,256]{3,2,1,0:T(8,128)(2,1)}, u32[]{:S(2)}, u32[]{:S(2)}) %all-to-all-start.2) | async-done | bytes 1048608 | tf_op jit(solution)/shard_map/all_to_all | solution.py:829
  217.9 1.6 copy-done.16
  219.5 11.8 %attention_backward.1 = bf16[8,2,128,512]{3,2,1,0:T(8,128)(2,1)S(1)} custom-call(s32[2,16]{1,0:T(2,128)S(1)} %select_reduce_fusion.order_ref, bf16[8,2,128,512]{3,2,1,0:T(8,128)(2,1)S(1)} %all-to-all-done.qkv_ref, bf16[8,2,128,256]{3,2,1,0:T(8,128)(2,1)} %all-to-all-done.2.grad_ref, f32[2,2,1024,128]{3,2,1,0:T(8,128)S(1)} %copy-done.16), custom_call_target="tpu_custom_call" | custom-call | flops 3400000000 | bytes 8388608 | tf_op jit(solution)/shard_map/attention_backward/pallas_call | solution.py:508
  231.3 1.3 copy-done.7
  232.6 4.2 all-to-all-start.3
  236.8 4.0 convolution_convert_fusion.2
  240.8 22.6 %all-to-all-done.3.grad_ref = bf16[8,2,128,512]{3,2,1,0:T(8,128)(2,1)S(1)} async-done(((bf16[8,2,128,512]{3,2,1,0:T(8,128)(2,1)}), bf16[8,2,128,512]{3,2,1,0:T(8,128)(2,1)S(1)}, u32[]{:S(2)}, u32[]{:S(2)}) %all-to-all-start.3) | async-done | bytes 2097184 | tf_op jit(solution)/shard_map/all_to_all | solution.py:829
  263.4 1.3 copy-done.2
  264.7 2.2 copy-done.1
  266.9 1.6 copy-done.3
  268.5 1.6 copy-done.5
  270.1 1.2 copy-done.8
  271.3 7.2 %last.1 = (bf16[256,1024]{1,0:T(8,128)(2,1)}, bf16[256,4096]{1,0:T(8,128)(2,1)S(1)}, f32[8,1024]{1,0:T(8,128)S(1)}) custom-call(s32[1]{0:T(128)} %bitcast.core_ref, bf16[8,2,128,512]{3,2,1,0:T(8,128)(2,1)S(1)} %copy-done.3, f32[256,2048]{1,0:T(8,128)S(1)} %copy-done.5, f32[256,1024]{1,0:T(8,128)S(1)} %get-tuple-element.57.k_raw_ref, ...), custom_call_target="tpu_custom_call" | custom-call | flops 2200000000 | bytes 16777216 | tf_op jit(solution)/shard_map/last/pallas_call | solution.py:757
  278.6 3.2 convolution_convert_fusion.1
  282.2 2.0 convolution_convert_fusion.3
  284.8 0.8 slice.38
  285.7 7.0 %collective-permute-done.5 = bf16[1024,1024]{1,0:T(8,128)(2,1)} collective-permute-done((bf16[1024,1024]{1,0:T(8,128)(2,1)}, bf16[1024,1024]{1,0:T(8,128)(2,1)}, u32[]{:S(2)}, u32[]{:S(2)}) %collective-permute-start.5) | collective-permute-done | bytes 2097184 | tf_op jit(solution)/shard_map/ppermute | solution.py:779
  292.7 2.5 add_convert_fusion.3
  295.3 4.8 %add_convert_fusion.2 = bf16[1536,1024]{1,0:T(8,128)(2,1)} fusion(bf16[1536,1024]{1,0:T(8,128)(2,1)} %collective-permute-done.7, bf16[1536,256]{1,0:T(8,128)(2,1)S(1)} %bitcast.63, bf16[256,1024]{1,0:T(8,128)(2,1)S(1)} %copy-done.19), kind=kOutput, calls=%fused_computation.3 | convolution fusion | flops 810024960 | bytes 7602176 | tf_op jit(solution)/shard_map/dot_general | solution.py:409
  300.1 7.3 %add_convert_fusion = bf16[512,6144]{1,0:T(8,128)(2,1)} fusion(bf16[512,6144]{1,0:T(8,128)(2,1)} %collective-permute-done.6, bf16[512,256]{1,0:T(8,128)(2,1)S(1)} %bitcast.66, bf16[256,6144]{1,0:T(8,128)(2,1)S(1)} %copy-done.17), kind=kOutput, calls=%fused_computation | convolution fusion | flops 1620049920 | bytes 15990784 | tf_op jit(solution)/shard_map/dot_general | solution.py:409
  307.4 5.4 %add_convert_fusion.1 = bf16[512,4096]{1,0:T(8,128)(2,1)} fusion(bf16[512,4096]{1,0:T(8,128)(2,1)} %collective-permute-done.4, bf16[512,256]{1,0:T(8,128)(2,1)S(1)} %bitcast.52, bf16[256,4096]{1,0:T(8,128)(2,1)S(1)} %get-tuple-element.61), kind=kOutput, calls=%fused_computation.2 | convolution fusion | flops 1080033280 | bytes 10747904 | tf_op jit(solution)/shard_map/dot_general | solution.py:409
  312.8 102.8 %reduce_grads.1 = (bf16[64,4096]{1,0:T(8,128)(2,1)S(1)}, bf16[128,1024]{1,0:T(8,128)(2,1)S(1)}, bf16[64,6144]{1,0:T(8,128)(2,1)S(1)}, bf16[192,1024]{1,0:T(8,128)(2,1)S(1)}, f32[8,1024]{1,0:T(8,128)S(1)}) custom-call(bf16[4,2,64,4096]{3,2,1,0:T(8,128)(2,1)} %bitcast.59, bf16[4,2,128,1024]{3,2,1,0:T(8,128)(2,1)S(1)} %bitcast.51, ...), custom_call_target="tpu_custom_call" | custom-call | tf_op jit(solution)/shard_map/reduce_grads/pallas_call | solution.py:389
  415.6 0.8 fusion.2
  416.5 0.8 slice.48
  417.3 1.3 fusion.1
  418.6 1.0 convert_element_type.75
  419.5 0.8 convert_element_type.73
  (67 shorter events, 6.6 us)
Async XLA Ops:
  87.5 7.6 %collective-permute-start = (bf16[8,64,4096]{2,1,0:T(8,128)(2,1)}, bf16[8,64,4096]{2,1,0:T(8,128)(2,1)}, u32[]{:S(2)}, u32[]{:S(2)}) collective-permute-start(bf16[8,64,4096]{2,1,0:T(8,128)(2,1)} %bitcast.48), channel_id=1, source_target_pairs={{0,1},{1,0},{2,3},{3,2},{4,5},{5,4},{6,7},{7,6},{8,9},{9,8},{10,11... | collective-permute-start | bytes 12582920 | tf_op jit(solution)/shard_map/ppermute | solution.py:779
  87.9 69.3 %collective-permute-start.2 = (bf16[8,64,6144]{2,1,0:T(8,128)(2,1)}, bf16[8,64,6144]{2,1,0:T(8,128)(2,1)}, u32[]{:S(2)}, u32[]{:S(2)}) collective-permute-start(bf16[8,64,6144]{2,1,0:T(8,128)(2,1)} %bitcast.74), channel_id=1, source_target_pairs={{0,1},{1,0},{2,3},{3,2},{4,5},{5,4},{6,7},{7,6},{8,9},{9,8},{10,11... | collective-permute-start | bytes 18874376 | tf_op jit(solution)/shard_map/ppermute | solution.py:779
  88.1 69.1 %collective-permute-start.3 = (bf16[8,192,1024]{2,1,0:T(8,128)(2,1)}, bf16[8,192,1024]{2,1,0:T(8,128)(2,1)}, u32[]{:S(2)}, u32[]{:S(2)}) collective-permute-start(bf16[8,192,1024]{2,1,0:T(8,128)(2,1)} %bitcast.76), channel_id=1, source_target_pairs={{0,1},{1,0},{2,3},{3,2},{4,5},{5,4},{6,7},{7,6},{8,9},{9,8},{10,11... | collective-permute-start | bytes 9437192 | tf_op jit(solution)/shard_map/ppermute | solution.py:779
  95.1 2.2 copy-start
  97.2 1.0 copy-start.12
  104.3 1.3 copy-start.4
  105.6 1.3 copy-start.6
  107.0 0.7 copy-start.10
  107.7 0.7 copy-start.13
  108.4 5.1 %copy-start.23 = (s32[2,16]{1,0:T(2,128)S(1)}, s32[2,16]{1,0:T(2,128)}, u32[]{:S(2)}) copy-start(s32[2,16]{1,0:T(2,128)} %param.15) | copy-start | bytes 388
  108.4 31.9 %all-to-all-start = ((bf16[8,2,128,512]{3,2,1,0:T(8,128)(2,1)}), bf16[8,2,128,512]{3,2,1,0:T(8,128)(2,1)S(1)}, u32[]{:S(2)}, u32[]{:S(2)}) async-start(bf16[8,2,128,512]{3,2,1,0:T(8,128)(2,1)} %copy-done.6), calls=%async_computation | async-start | bytes 4194304 | tf_op jit(solution)/shard_map/all_to_all | solution.py:829
  113.4 43.8 %collective-permute-start.1 = (bf16[8,128,1024]{2,1,0:T(8,128)(2,1)}, bf16[8,128,1024]{2,1,0:T(8,128)(2,1)}, u32[]{:S(2)}, u32[]{:S(2)}) collective-permute-start(bf16[8,128,1024]{2,1,0:T(8,128)(2,1)} %bitcast.78), channel_id=1, source_target_pairs={{0,1},{1,0},{2,3},{3,2},{4,5},{5,4},{6,7},{7,6},{8,9},{9,8},{10,11... | collective-permute-start | bytes 6291464 | tf_op jit(solution)/shard_map/ppermute | solution.py:779
  148.5 1.0 copy-start.9
  149.5 1.3 copy-start.15
  150.9 20.9 %all-to-all-start.1 = ((bf16[8,2,128,256]{3,2,1,0:T(8,128)(2,1)}), bf16[8,2,128,256]{3,2,1,0:T(8,128)(2,1)}, u32[]{:S(2)}, u32[]{:S(2)}) async-start(bf16[8,2,128,256]{3,2,1,0:T(8,128)(2,1)} %copy-done.9), calls=%async_computation.1 | async-start | bytes 2097152 | tf_op jit(solution)/shard_map/all_to_all | solution.py:829
  197.7 20.2 %all-to-all-start.2 = ((bf16[8,2,128,256]{3,2,1,0:T(8,128)(2,1)}), bf16[8,2,128,256]{3,2,1,0:T(8,128)(2,1)}, u32[]{:S(2)}, u32[]{:S(2)}) async-start(bf16[8,2,128,256]{3,2,1,0:T(8,128)(2,1)} %get-tuple-element.54), calls=%async_computation.2 | async-start | bytes 2097152 | tf_op jit(solution)/shard_map/all_to_all | solution.py:829
  208.4 91.7 %collective-permute-start.6 = (bf16[512,6144]{1,0:T(8,128)(2,1)}, bf16[512,6144]{1,0:T(8,128)(2,1)}, u32[]{:S(2)}, u32[]{:S(2)}) collective-permute-start(bf16[512,6144]{1,0:T(8,128)(2,1)} %convolution_convert_fusion), channel_id=1, source_target_pairs={{0,1},{1,0},{2,3},{3,2},{4,5},{5,4},{6,7},{7,6},{8,9},{9,8},{10,11... | collective-permute-start | bytes 18874376 | tf_op jit(solution)/shard_map/ppermute | solution.py:779
  217.9 1.6 copy-start.16
  231.3 1.3 copy-start.7
  232.6 30.8 %all-to-all-start.3 = ((bf16[8,2,128,512]{3,2,1,0:T(8,128)(2,1)}), bf16[8,2,128,512]{3,2,1,0:T(8,128)(2,1)S(1)}, u32[]{:S(2)}, u32[]{:S(2)}) async-start(bf16[8,2,128,512]{3,2,1,0:T(8,128)(2,1)} %copy-done.7), calls=%async_computation.3 | async-start | bytes 4194304 | tf_op jit(solution)/shard_map/all_to_all | solution.py:829
  240.8 54.5 %collective-permute-start.7 = (bf16[1536,1024]{1,0:T(8,128)(2,1)}, bf16[1536,1024]{1,0:T(8,128)(2,1)}, u32[]{:S(2)}, u32[]{:S(2)}) collective-permute-start(bf16[1536,1024]{1,0:T(8,128)(2,1)} %convolution_convert_fusion.2), channel_id=1, source_target_pairs={{0,1},{1,0},{2,3},{3,2},{4,5},{5,4},{6,7},{7,6},{8,9},{9,8},{10,11... | collective-permute-start | bytes 9437192 | tf_op jit(solution)/shard_map/ppermute | solution.py:779
  263.4 1.3 copy-start.2
  264.7 2.2 copy-start.1
  266.9 1.6 copy-start.3
  268.5 1.6 copy-start.5
  270.1 1.2 copy-start.8
  271.3 7.3 %copy-start.14 = (bf16[8,64,256]{2,1,0:T(8,128)(2,1)S(1)}, bf16[8,64,256]{2,1,0:T(8,128)(2,1)}, u32[]{:S(2)}) copy-start(bf16[8,64,256]{2,1,0:T(8,128)(2,1)} %copy-done.13) | copy-start | bytes 786436
  278.6 3.7 copy-start.18
  278.6 3.6 copy-start.21
  281.8 25.6 %collective-permute-start.4 = (bf16[512,4096]{1,0:T(8,128)(2,1)}, bf16[512,4096]{1,0:T(8,128)(2,1)}, u32[]{:S(2)}, u32[]{:S(2)}) collective-permute-start(bf16[512,4096]{1,0:T(8,128)(2,1)} %convolution_convert_fusion.1), channel_id=1, source_target_pairs={{0,1},{1,0},{2,3},{3,2},{4,5},{5,4},{6,7},{7,6},{8,9},{9,8},{10,11... | collective-permute-start | bytes 12582920 | tf_op jit(solution)/shard_map/ppermute | solution.py:779
  284.3 11.0 %copy-start.19 = (bf16[256,1024]{1,0:T(8,128)(2,1)S(1)}, bf16[256,1024]{1,0:T(8,128)(2,1)}, u32[]{:S(2)}) copy-start(bf16[256,1024]{1,0:T(8,128)(2,1)} %get-tuple-element.70) | copy-start | bytes 1572868
  284.3 8.4 %collective-permute-start.5 = (bf16[1024,1024]{1,0:T(8,128)(2,1)}, bf16[1024,1024]{1,0:T(8,128)(2,1)}, u32[]{:S(2)}, u32[]{:S(2)}) collective-permute-start(bf16[1024,1024]{1,0:T(8,128)(2,1)} %convolution_convert_fusion.3), channel_id=1, source_target_pairs={{0,1},{1,0},{2,3},{3,2},{4,5},{5,4},{6,7},{7,6},{8,9},{9,8},{10,11... | collective-permute-start | bytes 6291464 | tf_op jit(solution)/shard_map/ppermute | solution.py:779
  284.8 10.5 %copy-start.20 = (bf16[8,192,256]{2,1,0:T(8,128)(2,1)S(1)}, bf16[8,192,256]{2,1,0:T(8,128)(2,1)}, u32[]{:S(2)}) copy-start(bf16[8,192,256]{2,1,0:T(8,128)(2,1)} %get-tuple-element.69) | copy-start | bytes 2359300
  295.3 4.8 %copy-start.17 = (bf16[256,6144]{1,0:T(8,128)(2,1)S(1)}, bf16[256,6144]{1,0:T(8,128)(2,1)}, u32[]{:S(2)}) copy-start(bf16[256,6144]{1,0:T(8,128)(2,1)} %get-tuple-element.67) | copy-start | bytes 9437188
  295.3 4.8 %copy-start.22 = (bf16[8,64,256]{2,1,0:T(8,128)(2,1)S(1)}, bf16[8,64,256]{2,1,0:T(8,128)(2,1)}, u32[]{:S(2)}) copy-start(bf16[8,64,256]{2,1,0:T(8,128)(2,1)} %get-tuple-element.66) | copy-start | bytes 786436
  300.1 7.3 %copy-start.11 = (bf16[8,64,256]{2,1,0:T(8,128)(2,1)S(1)}, bf16[8,64,256]{2,1,0:T(8,128)(2,1)}, u32[]{:S(2)}) copy-start(bf16[8,64,256]{2,1,0:T(8,128)(2,1)} %copy-done.10) | copy-start | bytes 786436
